TPU v7x, 128 devices: a whole 4x4x4 slice. The times are simulated.
128 devices in a mesh: kvh: 8 (over z, x_hi), grp: 8 (over x_lo, y), blk: 2 (over core).
Axes of the slice: x: 4 (x_hi: 2, x_lo: 2; x = x_hi * 2 + x_lo), y: 4, z: 4, core: 2. Of those that a mesh axis runs over, the one named last changes fastest.
Arguments:
- queries: bfloat16 [32, 32, 16384], P(('grp', 'blk'), None, 'kvh'), may hold values from -30 to 30
- new_keys: bfloat16 [32, 32, 1024], P(('grp', 'blk'), None, 'kvh'), may hold values from -12 to 12
- new_values: bfloat16 [32, 32, 1024], P(('grp', 'blk'), None, 'kvh'), may hold values from -6 to 6
- prefix_keys: bfloat16 [16384, 1024], P(('grp', 'blk'), 'kvh'), may hold values from -8 to 8
- prefix_values: bfloat16 [16384, 1024], P(('grp', 'blk'), 'kvh'), may hold values from -6 to 6
- pool_keys: bfloat16 [512, 128, 1024], P(('grp', 'blk'), None, 'kvh'), may hold values from -7.1875 to 7.1875
- pool_values: bfloat16 [512, 128, 1024], P(('grp', 'blk'), None, 'kvh'), may hold values from -6 to 6
- hist_blocks: int32 [32, 16], replicated, may hold values from 0 to 511, as said below
- hist_len: int32 [32], replicated, may hold values from 1 to 2048
- out_weight: bfloat16 [16384, 16384], P('kvh', ('grp', 'blk')), may hold values from -0.046875 to 0.046875
Outputs:
- heads_out: bfloat16 [32, 32, 16384], P(('grp', 'blk'), None, 'kvh')
- projected: bfloat16 [32, 32, 16384], P('kvh', None, ('grp', 'blk'))
Inputs may be any that keep to these rules, and one draw needn't show every extreme that they name: `hist_blocks`: block id b is row b mod 32 of the pool held by device b // 32 along grp+blk (grp slowest). Every pool block is named exactly once. The 2 requests placed on one device along grp+blk name exactly 2 blocks held by each device along grp+blk.
All inputs are finite; a program needn't handle non-finite values.
Results may differ from a plain program's by a relative error of at most 0.017.
Values may be sent and summed in bfloat16 or wider, within the bound.
A program may use at most 192 MiB of HBM per device.

v0:
```python
import jax
import jax.numpy as jnp
from jax import lax
from jax.sharding import PartitionSpec as P


def from_behind(block, axis, distance):
    devices = range(lax.axis_size(axis))
    route = [((i - distance) % len(devices), i) for i in devices]
    return lax.ppermute(block, axis, route)


def absorb(query_rows, carried, keys, values, factor):
    top_score, total, accum = carried
    scores = jnp.dot(query_rows, keys.T, preferred_element_type=jnp.float32) * factor
    newest = jnp.maximum(top_score, jnp.max(scores, axis=1))
    shrink = jnp.exp(top_score - newest)
    weights = jnp.exp(scores - newest[:, None])
    total = total * shrink + jnp.sum(weights, axis=1)
    accum = accum * shrink[:, None] + jnp.dot(
        weights.astype(jnp.bfloat16), values, preferred_element_type=jnp.float32
    )
    return (newest, total, accum)


def on_device(
    queries,
    new_keys,
    new_values,
    prefix_keys,
    prefix_values,
    pool_keys,
    pool_values,
    hist_blocks,
    hist_len,
    out_weight,
):
    holders = lax.axis_size(("grp", "blk"))
    myself = lax.axis_index(("grp", "blk"))
    local_reqs, new_tok, width = queries.shape
    head_dim = prefix_keys.shape[1]
    groups = width // head_dim
    factor = head_dim ** (-0.5)
    row_count = local_reqs * new_tok * groups
    query_rows = queries.reshape(row_count, head_dim)
    start_state = (
        jnp.full((row_count,), -1e30, jnp.float32),
        jnp.zeros((row_count,), jnp.float32),
        jnp.zeros((row_count, head_dim), jnp.float32),
    )

    def pass_turn(step_index, loop_state):
        key_values, carried = loop_state
        carried = absorb(query_rows, carried, key_values[0], key_values[1], factor)
        key_values = from_behind(key_values, ("grp", "blk"), 1)
        return (key_values, carried)

    stacked = jnp.stack([prefix_keys, prefix_values])
    stacked, carried = lax.fori_loop(0, holders - 1, pass_turn, (stacked, start_state))
    carried = absorb(query_rows, carried, stacked[0], stacked[1], factor)
    block_count = hist_blocks.shape[1]
    slot_count = local_reqs * block_count
    pool_dev = pool_keys.shape[0]
    per_holder = slot_count // holders
    block_size = pool_keys.shape[1]
    all_ids = hist_blocks.reshape(holders, slot_count)
    owners = all_ids // pool_dev
    positions = jnp.arange(slot_count, dtype=jnp.int32)
    ranked = jnp.argsort(
        jnp.where(owners == myself, positions[None, :], positions[None, :] + slot_count),
        axis=1,
        stable=True,
    )[:, :per_holder]
    local_ids = jnp.take_along_axis(all_ids, ranked, axis=1) - myself * pool_dev
    got_keys, got_values = (
        lax.all_to_all(
            pool_keys[local_ids], ("grp", "blk"), split_axis=0, concat_axis=0, tiled=True
        ),
        lax.all_to_all(
            pool_values[local_ids], ("grp", "blk"), split_axis=0, concat_axis=0, tiled=True
        ),
    )
    my_ids = lax.dynamic_slice_in_dim(all_ids, myself, 1, 0)[0]
    my_owners = my_ids // pool_dev
    earlier = (my_owners[:, None] == my_owners[None, :]) & (positions[None, :] < positions[:, None])
    arrival = my_owners * per_holder + jnp.sum(earlier.astype(jnp.int32), axis=1)
    hist_length = block_count * block_size
    past_keys = got_keys.reshape(holders * per_holder, block_size, head_dim)[arrival].reshape(
        local_reqs, hist_length, head_dim
    )
    past_values = got_values.reshape(holders * per_holder, block_size, head_dim)[arrival].reshape(
        local_reqs, hist_length, head_dim
    )
    lengths = lax.dynamic_slice_in_dim(hist_len, myself * local_reqs, local_reqs)
    near_keys = jnp.concatenate([past_keys, new_keys], axis=1)
    near_values = jnp.concatenate([past_values, new_values], axis=1)
    grouped = queries.reshape(local_reqs, new_tok * groups, head_dim)
    near_scores = (
        jnp.einsum("rqd,rkd->rqk", grouped, near_keys, preferred_element_type=jnp.float32) * factor
    )
    key_pos = jnp.arange(hist_length + new_tok, dtype=jnp.int32)
    query_tok = jnp.arange(new_tok * groups, dtype=jnp.int32) // groups
    past_ok = (key_pos[None, :] < hist_length) & (key_pos[None, :] < lengths[:, None])
    own_ok = (key_pos[None, :] >= hist_length) & (
        key_pos[None, :] - hist_length <= query_tok[:, None]
    )
    visible = past_ok[:, None, :] | own_ok[None, :, :]
    near_scores = jnp.where(visible, near_scores, jnp.float32(-1e30))
    near_top = jnp.max(near_scores, axis=2)
    near_weights = jnp.where(visible, jnp.exp(near_scores - near_top[:, :, None]), jnp.float32(0.0))
    near_total = jnp.sum(near_weights, axis=2)
    near_sum = jnp.einsum(
        "rqk,rkd->rqd",
        near_weights.astype(jnp.bfloat16),
        near_values,
        preferred_element_type=jnp.float32,
    )
    far_top = carried[0].reshape(local_reqs, new_tok * groups)
    far_total = carried[1].reshape(local_reqs, new_tok * groups)
    far_sum = carried[2].reshape(local_reqs, new_tok * groups, head_dim)
    best_top = jnp.maximum(far_top, near_top)
    far_ratio = jnp.exp(far_top - best_top)
    near_ratio = jnp.exp(near_top - best_top)
    combined = (far_sum * far_ratio[:, :, None] + near_sum * near_ratio[:, :, None]) / (
        far_total * far_ratio + near_total * near_ratio
    )[:, :, None]
    heads_out = combined.astype(jnp.bfloat16).reshape(local_reqs, new_tok, width)
    out_cols = out_weight.shape[1]
    shard_piece = lax.all_gather(heads_out, ("grp", "blk"), axis=0, tiled=True)
    flat = jnp.dot(shard_piece.reshape(-1, width), out_weight, preferred_element_type=jnp.float32)
    terms = flat.reshape(shard_piece.shape[0], new_tok, out_cols)
    projected = lax.psum_scatter(terms.astype(jnp.bfloat16), "kvh", scatter_dimension=0, tiled=True)
    return (heads_out, projected)


def solution(mesh):
    in_specs = (
        P(("grp", "blk"), None, "kvh"),
        P(("grp", "blk"), None, "kvh"),
        P(("grp", "blk"), None, "kvh"),
        P(("grp", "blk"), "kvh"),
        P(("grp", "blk"), "kvh"),
        P(("grp", "blk"), None, "kvh"),
        P(("grp", "blk"), None, "kvh"),
        P(),
        P(),
        P("kvh", ("grp", "blk")),
    )
    out_specs = (P(("grp", "blk"), None, "kvh"), P("kvh", None, ("grp", "blk")))
    return jax.shard_map(
        on_device, mesh=mesh, in_specs=in_specs, out_specs=out_specs, check_vma=False
    )
```

profile of v0, /device:TPU:18, one launch (start us, length us, event | category | flops | bytes accessed | tf_op | source)
XLA Modules:
  0.0 362.4 jit_solution(14713335830030291652)
XLA Ops:
  7.2 0.9 copy.30
  8.3 0.8 sort.17
  10.4 1.7 gather_fusion.2
  12.1 5.7 %all-to-all-start.1 = ((bf16[16,2,128,128]{3,2,1,0:T(8,128)(2,1)}), bf16[16,2,128,128]{3,2,1,0:T(8,128)(2,1)}, u32[]{:S(2)}, u32[]{:S(2)}) async-start(bf16[16,2,128,128]{3,2,1,0:T(8,128)(2,1)} %bitcast.15), calls=%async_computation.1 | async-start | bytes 2097152 | tf_op jit(solution)/shard_map/all_to_all | solution.py:79
  18.0 0.8 reshape.304
  19.1 1.7 gather_fusion
  20.8 1.1 pad_maximum_fusion
  21.8 145.6 %while.17 = (s32[]{:T(128)}, bf16[2,1024,128]{2,1,0:T(8,128)(2,1)S(1)}, f32[1024]{0:T(1024)S(1)}, f32[1024]{0:T(1024)S(1)}, f32[1024,128]{1,0:T(8,128)S(1)}, /*i...) while((s32[]{:T(128)}, bf16[2,1024,128]{2,1,0:T(8,128)(2,1)S(1)}, f32[1024]{0:T(1024)S(1)}, ...), condition=%wide.region_3.0_spmd.clone, body=%wide.region_0.0_spmd.clone.sunk | while | flops 545657856 | bytes 17629320 | solution.py:59
  22.8 0.7 fusion.98
  23.6 1.0 fusion.100
  24.6 11.8 %collective-permute-done = bf16[2,1024,128]{2,1,0:T(8,128)(2,1)S(1)} collective-permute-done((bf16[2,1024,128]{2,1,0:T(8,128)(2,1)S(1)}, bf16[2,1024,128]{2,1,0:T(8,128)(2,1)S(1)}, u32[]{:S(2)}, u32[]{:S(2)}) %collective-permute-start) | collective-permute-done | bytes 524320 | tf_op jit(solution)/shard_map/while/body/eval_jaxpr/ppermute | solution.py:10
  37.3 0.7 fusion.98
  38.0 1.0 fusion.100
  39.0 6.1 %collective-permute-done = bf16[2,1024,128]{2,1,0:T(8,128)(2,1)S(1)} collective-permute-done((bf16[2,1024,128]{2,1,0:T(8,128)(2,1)S(1)}, bf16[2,1024,128]{2,1,0:T(8,128)(2,1)S(1)}, u32[]{:S(2)}, u32[]{:S(2)}) %collective-permute-start) | collective-permute-done | bytes 524320 | tf_op jit(solution)/shard_map/while/body/eval_jaxpr/ppermute | solution.py:10
  46.0 0.7 fusion.98
  46.7 1.0 fusion.100
  47.7 6.1 %collective-permute-done = bf16[2,1024,128]{2,1,0:T(8,128)(2,1)S(1)} collective-permute-done((bf16[2,1024,128]{2,1,0:T(8,128)(2,1)S(1)}, bf16[2,1024,128]{2,1,0:T(8,128)(2,1)S(1)}, u32[]{:S(2)}, u32[]{:S(2)}) %collective-permute-start) | collective-permute-done | bytes 524320 | tf_op jit(solution)/shard_map/while/body/eval_jaxpr/ppermute | solution.py:10
  54.7 0.7 fusion.98
  55.5 1.0 fusion.100
  56.5 6.1 %collective-permute-done = bf16[2,1024,128]{2,1,0:T(8,128)(2,1)S(1)} collective-permute-done((bf16[2,1024,128]{2,1,0:T(8,128)(2,1)S(1)}, bf16[2,1024,128]{2,1,0:T(8,128)(2,1)S(1)}, u32[]{:S(2)}, u32[]{:S(2)}) %collective-permute-start) | collective-permute-done | bytes 524320 | tf_op jit(solution)/shard_map/while/body/eval_jaxpr/ppermute | solution.py:10
  63.4 0.7 fusion.98
  64.2 1.0 fusion.100
  65.2 6.1 %collective-permute-done = bf16[2,1024,128]{2,1,0:T(8,128)(2,1)S(1)} collective-permute-done((bf16[2,1024,128]{2,1,0:T(8,128)(2,1)S(1)}, bf16[2,1024,128]{2,1,0:T(8,128)(2,1)S(1)}, u32[]{:S(2)}, u32[]{:S(2)}) %collective-permute-start) | collective-permute-done | bytes 524320 | tf_op jit(solution)/shard_map/while/body/eval_jaxpr/ppermute | solution.py:10
  72.1 0.7 fusion.98
  72.9 1.0 fusion.100
  73.9 6.1 %collective-permute-done = bf16[2,1024,128]{2,1,0:T(8,128)(2,1)S(1)} collective-permute-done((bf16[2,1024,128]{2,1,0:T(8,128)(2,1)S(1)}, bf16[2,1024,128]{2,1,0:T(8,128)(2,1)S(1)}, u32[]{:S(2)}, u32[]{:S(2)}) %collective-permute-start) | collective-permute-done | bytes 524320 | tf_op jit(solution)/shard_map/while/body/eval_jaxpr/ppermute | solution.py:10
  80.8 0.7 fusion.98
  81.6 1.0 fusion.100
  82.6 6.1 %collective-permute-done = bf16[2,1024,128]{2,1,0:T(8,128)(2,1)S(1)} collective-permute-done((bf16[2,1024,128]{2,1,0:T(8,128)(2,1)S(1)}, bf16[2,1024,128]{2,1,0:T(8,128)(2,1)S(1)}, u32[]{:S(2)}, u32[]{:S(2)}) %collective-permute-start) | collective-permute-done | bytes 524320 | tf_op jit(solution)/shard_map/while/body/eval_jaxpr/ppermute | solution.py:10
  89.9 0.7 fusion.98
  90.7 1.0 fusion.100
  91.7 5.7 %collective-permute-done = bf16[2,1024,128]{2,1,0:T(8,128)(2,1)S(1)} collective-permute-done((bf16[2,1024,128]{2,1,0:T(8,128)(2,1)S(1)}, bf16[2,1024,128]{2,1,0:T(8,128)(2,1)S(1)}, u32[]{:S(2)}, u32[]{:S(2)}) %collective-permute-start) | collective-permute-done | bytes 524320 | tf_op jit(solution)/shard_map/while/body/eval_jaxpr/ppermute | solution.py:10
  97.5 2.6 collective-permute-start
  100.7 0.7 fusion.98
  101.5 1.0 fusion.100
  102.5 3.6 %collective-permute-done = bf16[2,1024,128]{2,1,0:T(8,128)(2,1)S(1)} collective-permute-done((bf16[2,1024,128]{2,1,0:T(8,128)(2,1)S(1)}, bf16[2,1024,128]{2,1,0:T(8,128)(2,1)S(1)}, u32[]{:S(2)}, u32[]{:S(2)}) %collective-permute-start) | collective-permute-done | bytes 524320 | tf_op jit(solution)/shard_map/while/body/eval_jaxpr/ppermute | solution.py:10
  106.2 4.7 %collective-permute-start = (bf16[2,1024,128]{2,1,0:T(8,128)(2,1)S(1)}, bf16[2,1024,128]{2,1,0:T(8,128)(2,1)S(1)}, u32[]{:S(2)}, u32[]{:S(2)}) collective-permute-start(bf16[2,1024,128]{2,1,0:T(8,128)(2,1)S(1)} %copy.44), channel_id=1, source_target_pairs={{15,0},{0,1},{1,2},{2,3},{3,4},{4,5},{5,6},{6,7},{7,8},{8,9},{9,10... | collective-permute-start | bytes 1572872 | tf_op jit(solution)/shard_map/while/body/eval_jaxpr/ppermute | solution.py:10
  112.3 1.0 fusion.100
  113.3 1.5 collective-permute-done
  114.9 6.8 %collective-permute-start = (bf16[2,1024,128]{2,1,0:T(8,128)(2,1)S(1)}, bf16[2,1024,128]{2,1,0:T(8,128)(2,1)S(1)}, u32[]{:S(2)}, u32[]{:S(2)}) collective-permute-start(bf16[2,1024,128]{2,1,0:T(8,128)(2,1)S(1)} %copy.44), channel_id=1, source_target_pairs={{15,0},{0,1},{1,2},{2,3},{3,4},{4,5},{5,6},{6,7},{7,8},{8,9},{9,10... | collective-permute-start | bytes 1572872 | tf_op jit(solution)/shard_map/while/body/eval_jaxpr/ppermute | solution.py:10
  123.1 1.0 fusion.100
  124.2 8.3 %collective-permute-start = (bf16[2,1024,128]{2,1,0:T(8,128)(2,1)S(1)}, bf16[2,1024,128]{2,1,0:T(8,128)(2,1)S(1)}, u32[]{:S(2)}, u32[]{:S(2)}) collective-permute-start(bf16[2,1024,128]{2,1,0:T(8,128)(2,1)S(1)} %copy.44), channel_id=1, source_target_pairs={{15,0},{0,1},{1,2},{2,3},{3,4},{4,5},{5,6},{6,7},{7,8},{8,9},{9,10... | collective-permute-start | bytes 1572872 | tf_op jit(solution)/shard_map/while/body/eval_jaxpr/ppermute | solution.py:10
  134.0 1.0 fusion.100
  135.0 8.3 %collective-permute-start = (bf16[2,1024,128]{2,1,0:T(8,128)(2,1)S(1)}, bf16[2,1024,128]{2,1,0:T(8,128)(2,1)S(1)}, u32[]{:S(2)}, u32[]{:S(2)}) collective-permute-start(bf16[2,1024,128]{2,1,0:T(8,128)(2,1)S(1)} %copy.44), channel_id=1, source_target_pairs={{15,0},{0,1},{1,2},{2,3},{3,4},{4,5},{5,6},{6,7},{7,8},{8,9},{9,10... | collective-permute-start | bytes 1572872 | tf_op jit(solution)/shard_map/while/body/eval_jaxpr/ppermute | solution.py:10
  144.8 1.0 fusion.100
  145.8 8.3 %collective-permute-start = (bf16[2,1024,128]{2,1,0:T(8,128)(2,1)S(1)}, bf16[2,1024,128]{2,1,0:T(8,128)(2,1)S(1)}, u32[]{:S(2)}, u32[]{:S(2)}) collective-permute-start(bf16[2,1024,128]{2,1,0:T(8,128)(2,1)S(1)} %copy.44), channel_id=1, source_target_pairs={{15,0},{0,1},{1,2},{2,3},{3,4},{4,5},{5,6},{6,7},{7,8},{8,9},{9,10... | collective-permute-start | bytes 1572872 | tf_op jit(solution)/shard_map/while/body/eval_jaxpr/ppermute | solution.py:10
  155.6 1.0 fusion.100
  156.7 8.3 %collective-permute-start = (bf16[2,1024,128]{2,1,0:T(8,128)(2,1)S(1)}, bf16[2,1024,128]{2,1,0:T(8,128)(2,1)S(1)}, u32[]{:S(2)}, u32[]{:S(2)}) collective-permute-start(bf16[2,1024,128]{2,1,0:T(8,128)(2,1)S(1)} %copy.44), channel_id=1, source_target_pairs={{15,0},{0,1},{1,2},{2,3},{3,4},{4,5},{5,6},{6,7},{7,8},{8,9},{9,10... | collective-permute-start | bytes 1572872 | tf_op jit(solution)/shard_map/while/body/eval_jaxpr/ppermute | solution.py:10
  166.4 1.0 fusion.100
  167.5 2.6 multiply_reduce_fusion.1
  170.1 2.9 fusion.25
  173.3 28.3 %all-to-all-start = ((bf16[16,2,128,128]{3,2,1,0:T(8,128)(2,1)}), bf16[16,2,128,128]{3,2,1,0:T(8,128)(2,1)}, u32[]{:S(2)}, u32[]{:S(2)}) async-start(bf16[16,2,128,128]{3,2,1,0:T(8,128)(2,1)} %bitcast.6), calls=%async_computation | async-start | bytes 2097152 | tf_op jit(solution)/shard_map/all_to_all | solution.py:76
  201.8 3.9 %fusion.34 = f32[1024,128]{1,0:T(8,128)} fusion(f32[1024,1024]{1,0:T(8,128)} %get-tuple-element.88, f32[1024]{0:T(1024)S(1)} %max.19, f32[1024,128]{1,0:T(8,128)S(1)} %get-tuple-element.38, bf16[2,1024,128]{2,1,0:T(8,128)(2,1)S(1)} %get-tuple-element.40, f32[1024]{0:T(1024)S(1)} %get-tuple-element.82), kind=kOutput, calls=%fused_computation.43 | convolution fusion | flops 271843328 | bytes 5513216 | tf_op jit(solution)/shard_map/dot_general | solution.py:20
  205.7 1.5 compare_and_fusion
  207.3 2.0 gather_fusion.3
  209.3 6.0 %all-to-all-done = bf16[16,2,128,128]{3,2,1,0:T(8,128)(2,1)} async-done(((bf16[16,2,128,128]{3,2,1,0:T(8,128)(2,1)}), bf16[16,2,128,128]{3,2,1,0:T(8,128)(2,1)}, u32[]{:S(2)}, u32[]{:S(2)}) %all-to-all-start) | async-done | bytes 1048608 | tf_op jit(solution)/shard_map/all_to_all | solution.py:76
  215.3 2.9 gather_fusion.1
  218.2 5.2 %fusion.16 = (f32[2,512]{1,0:T(2,128)S(1)}, f32[2,2080,512]{2,1,0:T(8,128)S(1)}) fusion(pred[512,2080]{0,1:T(8,128)(4,1)S(1)} %compare_and_fusion, pred[2,2080]{1,0:T(4,128)(4,1)S(1)} %compare_and_fusion.1, bf16[2,512,128]{2,1,0:T(8,128)(2,1)S(1)} %copy-done.4, bf16[2,32,128]{2,1,0:T(8,128)(2,1)S(1)} %copy-done.5, bf16[2,2048,128]{2,1,0:T(8,128)(2,1)} %bitcast.90), kind=kOutput, calls=%fused_computation.26 | convolution fusion | flops 555908096 | bytes 10920000 | tf_op jit(solution)/shard_map/rqd,rkd->rqk/dot_general | solution.py:99
  223.4 3.0 fusion.17
  226.5 4.1 %fusion.55 = bf16[2,512,128]{2,1,0:T(8,128)(2,1)S(1)} fusion(bf16[2,32,128]{2,1,0:T(8,128)(2,1)S(1)} %copy-done.6, bf16[2,2048,128]{2,1,0:T(8,128)(2,1)S(1)} %bitcast.89, f32[2,2080,512]{2,1,0:T(8,128)S(1)} %get-tuple-element.86, f32[2,512]{1,0:T(2,128)S(1)} %get-tuple-element.85, pred[512,2080]{0,1:T(8,128)(4,1)S(1)} %compare_and_fusion, ...), kind=kOutput, calls=%fused_computation.54 | convolution fusion | flops 560824320 | bytes 11456576 | tf_op jit(solution)/shard_map/rqk,rkd->rqd/dot_general | solution.py:112
  230.6 0.8 reshape.308
  231.5 39.2 %all-gather.2.cloned.1.call-done = bf16[32,32,2048]{2,1,0:T(8,128)(2,1)} async-done(((bf16[2,32,2048]{2,1,0:T(8,128)(2,1)}), bf16[32,32,2048]{2,1,0:T(8,128)(2,1)}) %all-gather.2.cloned.1.call-update) | async-done | bytes 4194320 | tf_op jit(solution)/shard_map/all_gather | solution.py:129
  270.7 9.3 %fusion.31 = bf16[32,32,1024]{2,1,0:T(8,128)(2,1)} fusion(bf16[32,32,2048]{2,1,0:T(8,128)(2,1)} %all-gather.2.cloned.1.call-done, bf16[2048,1024]{1,0:T(8,128)(2,1)} %param.21), kind=kOutput, calls=%fused_computation.42 | convolution fusion | flops 4296015872 | bytes 10485760 | tf_op jit(solution)/shard_map/dot_general | solution.py:130
  280.0 75.6 %reduce-scatter.2.cloned.1.call-done = bf16[4,32,1024]{2,1,0:T(8,128)(2,1)} async-done(((bf16[32,32,1024]{2,1,0:T(8,128)(2,1)}), bf16[4,32,1024]{2,1,0:T(8,128)(2,1)}) %reduce-scatter.2.cloned.1.call-update) | async-done | bytes 262160 | tf_op jit(solution)/shard_map/reduce_scatter | solution.py:132
  (150 shorter events, 19.5 us)
Async XLA Ops:
  7.2 3.2 copy-start
  10.0 7.9 %copy-start.2 = (bf16[2,32,2048]{2,1,0:T(8,128)(2,1)S(1)}, bf16[2,32,2048]{2,1,0:T(8,128)(2,1)}, u32[]{:S(2)}) copy-start(bf16[2,32,2048]{2,1,0:T(8,128)(2,1)} %param.12) | copy-start | bytes 786436
  10.0 9.1 %copy-start.1 = (bf16[32,128,128]{2,1,0:T(8,128)(2,1)S(1)}, bf16[32,128,128]{2,1,0:T(8,128)(2,1)}, u32[]{:S(2)}) copy-start(bf16[32,128,128]{2,1,0:T(8,128)(2,1)} %param.17) | copy-start | bytes 3145732
  12.1 161.2 %all-to-all-start.1 = ((bf16[16,2,128,128]{3,2,1,0:T(8,128)(2,1)}), bf16[16,2,128,128]{3,2,1,0:T(8,128)(2,1)}, u32[]{:S(2)}, u32[]{:S(2)}) async-start(bf16[16,2,128,128]{3,2,1,0:T(8,128)(2,1)} %bitcast.15), calls=%async_computation.1 | async-start | bytes 2097152 | tf_op jit(solution)/shard_map/all_to_all | solution.py:79
  21.9 14.5 %collective-permute-start = (bf16[2,1024,128]{2,1,0:T(8,128)(2,1)S(1)}, bf16[2,1024,128]{2,1,0:T(8,128)(2,1)S(1)}, u32[]{:S(2)}, u32[]{:S(2)}) collective-permute-start(bf16[2,1024,128]{2,1,0:T(8,128)(2,1)S(1)} %copy.44), channel_id=1, source_target_pairs={{15,0},{0,1},{1,2},{2,3},{3,4},{4,5},{5,6},{6,7},{7,8},{8,9},{9,10... | collective-permute-start | bytes 1572872 | tf_op jit(solution)/shard_map/while/body/eval_jaxpr/ppermute | solution.py:10
  36.5 8.7 %collective-permute-start = (bf16[2,1024,128]{2,1,0:T(8,128)(2,1)S(1)}, bf16[2,1024,128]{2,1,0:T(8,128)(2,1)S(1)}, u32[]{:S(2)}, u32[]{:S(2)}) collective-permute-start(bf16[2,1024,128]{2,1,0:T(8,128)(2,1)S(1)} %copy.44), channel_id=1, source_target_pairs={{15,0},{0,1},{1,2},{2,3},{3,4},{4,5},{5,6},{6,7},{7,8},{8,9},{9,10... | collective-permute-start | bytes 1572872 | tf_op jit(solution)/shard_map/while/body/eval_jaxpr/ppermute | solution.py:10
  45.2 8.7 %collective-permute-start = (bf16[2,1024,128]{2,1,0:T(8,128)(2,1)S(1)}, bf16[2,1024,128]{2,1,0:T(8,128)(2,1)S(1)}, u32[]{:S(2)}, u32[]{:S(2)}) collective-permute-start(bf16[2,1024,128]{2,1,0:T(8,128)(2,1)S(1)} %copy.44), channel_id=1, source_target_pairs={{15,0},{0,1},{1,2},{2,3},{3,4},{4,5},{5,6},{6,7},{7,8},{8,9},{9,10... | collective-permute-start | bytes 1572872 | tf_op jit(solution)/shard_map/while/body/eval_jaxpr/ppermute | solution.py:10
  53.9 8.7 %collective-permute-start = (bf16[2,1024,128]{2,1,0:T(8,128)(2,1)S(1)}, bf16[2,1024,128]{2,1,0:T(8,128)(2,1)S(1)}, u32[]{:S(2)}, u32[]{:S(2)}) collective-permute-start(bf16[2,1024,128]{2,1,0:T(8,128)(2,1)S(1)} %copy.44), channel_id=1, source_target_pairs={{15,0},{0,1},{1,2},{2,3},{3,4},{4,5},{5,6},{6,7},{7,8},{8,9},{9,10... | collective-permute-start | bytes 1572872 | tf_op jit(solution)/shard_map/while/body/eval_jaxpr/ppermute | solution.py:10
  62.6 8.7 %collective-permute-start = (bf16[2,1024,128]{2,1,0:T(8,128)(2,1)S(1)}, bf16[2,1024,128]{2,1,0:T(8,128)(2,1)S(1)}, u32[]{:S(2)}, u32[]{:S(2)}) collective-permute-start(bf16[2,1024,128]{2,1,0:T(8,128)(2,1)S(1)} %copy.44), channel_id=1, source_target_pairs={{15,0},{0,1},{1,2},{2,3},{3,4},{4,5},{5,6},{6,7},{7,8},{8,9},{9,10... | collective-permute-start | bytes 1572872 | tf_op jit(solution)/shard_map/while/body/eval_jaxpr/ppermute | solution.py:10
  71.3 8.7 %collective-permute-start = (bf16[2,1024,128]{2,1,0:T(8,128)(2,1)S(1)}, bf16[2,1024,128]{2,1,0:T(8,128)(2,1)S(1)}, u32[]{:S(2)}, u32[]{:S(2)}) collective-permute-start(bf16[2,1024,128]{2,1,0:T(8,128)(2,1)S(1)} %copy.44), channel_id=1, source_target_pairs={{15,0},{0,1},{1,2},{2,3},{3,4},{4,5},{5,6},{6,7},{7,8},{8,9},{9,10... | collective-permute-start | bytes 1572872 | tf_op jit(solution)/shard_map/while/body/eval_jaxpr/ppermute | solution.py:10
  80.0 8.7 %collective-permute-start = (bf16[2,1024,128]{2,1,0:T(8,128)(2,1)S(1)}, bf16[2,1024,128]{2,1,0:T(8,128)(2,1)S(1)}, u32[]{:S(2)}, u32[]{:S(2)}) collective-permute-start(bf16[2,1024,128]{2,1,0:T(8,128)(2,1)S(1)} %copy.44), channel_id=1, source_target_pairs={{15,0},{0,1},{1,2},{2,3},{3,4},{4,5},{5,6},{6,7},{7,8},{8,9},{9,10... | collective-permute-start | bytes 1572872 | tf_op jit(solution)/shard_map/while/body/eval_jaxpr/ppermute | solution.py:10
  88.7 8.7 %collective-permute-start = (bf16[2,1024,128]{2,1,0:T(8,128)(2,1)S(1)}, bf16[2,1024,128]{2,1,0:T(8,128)(2,1)S(1)}, u32[]{:S(2)}, u32[]{:S(2)}) collective-permute-start(bf16[2,1024,128]{2,1,0:T(8,128)(2,1)S(1)} %copy.44), channel_id=1, source_target_pairs={{15,0},{0,1},{1,2},{2,3},{3,4},{4,5},{5,6},{6,7},{7,8},{8,9},{9,10... | collective-permute-start | bytes 1572872 | tf_op jit(solution)/shard_map/while/body/eval_jaxpr/ppermute | solution.py:10
  97.5 8.7 %collective-permute-start = (bf16[2,1024,128]{2,1,0:T(8,128)(2,1)S(1)}, bf16[2,1024,128]{2,1,0:T(8,128)(2,1)S(1)}, u32[]{:S(2)}, u32[]{:S(2)}) collective-permute-start(bf16[2,1024,128]{2,1,0:T(8,128)(2,1)S(1)} %copy.44), channel_id=1, source_target_pairs={{15,0},{0,1},{1,2},{2,3},{3,4},{4,5},{5,6},{6,7},{7,8},{8,9},{9,10... | collective-permute-start | bytes 1572872 | tf_op jit(solution)/shard_map/while/body/eval_jaxpr/ppermute | solution.py:10
  106.2 8.7 %collective-permute-start = (bf16[2,1024,128]{2,1,0:T(8,128)(2,1)S(1)}, bf16[2,1024,128]{2,1,0:T(8,128)(2,1)S(1)}, u32[]{:S(2)}, u32[]{:S(2)}) collective-permute-start(bf16[2,1024,128]{2,1,0:T(8,128)(2,1)S(1)} %copy.44), channel_id=1, source_target_pairs={{15,0},{0,1},{1,2},{2,3},{3,4},{4,5},{5,6},{6,7},{7,8},{8,9},{9,10... | collective-permute-start | bytes 1572872 | tf_op jit(solution)/shard_map/while/body/eval_jaxpr/ppermute | solution.py:10
  114.9 9.3 %collective-permute-start = (bf16[2,1024,128]{2,1,0:T(8,128)(2,1)S(1)}, bf16[2,1024,128]{2,1,0:T(8,128)(2,1)S(1)}, u32[]{:S(2)}, u32[]{:S(2)}) collective-permute-start(bf16[2,1024,128]{2,1,0:T(8,128)(2,1)S(1)} %copy.44), channel_id=1, source_target_pairs={{15,0},{0,1},{1,2},{2,3},{3,4},{4,5},{5,6},{6,7},{7,8},{8,9},{9,10... | collective-permute-start | bytes 1572872 | tf_op jit(solution)/shard_map/while/body/eval_jaxpr/ppermute | solution.py:10
  124.2 10.8 %collective-permute-start = (bf16[2,1024,128]{2,1,0:T(8,128)(2,1)S(1)}, bf16[2,1024,128]{2,1,0:T(8,128)(2,1)S(1)}, u32[]{:S(2)}, u32[]{:S(2)}) collective-permute-start(bf16[2,1024,128]{2,1,0:T(8,128)(2,1)S(1)} %copy.44), channel_id=1, source_target_pairs={{15,0},{0,1},{1,2},{2,3},{3,4},{4,5},{5,6},{6,7},{7,8},{8,9},{9,10... | collective-permute-start | bytes 1572872 | tf_op jit(solution)/shard_map/while/body/eval_jaxpr/ppermute | solution.py:10
  135.0 10.8 %collective-permute-start = (bf16[2,1024,128]{2,1,0:T(8,128)(2,1)S(1)}, bf16[2,1024,128]{2,1,0:T(8,128)(2,1)S(1)}, u32[]{:S(2)}, u32[]{:S(2)}) collective-permute-start(bf16[2,1024,128]{2,1,0:T(8,128)(2,1)S(1)} %copy.44), channel_id=1, source_target_pairs={{15,0},{0,1},{1,2},{2,3},{3,4},{4,5},{5,6},{6,7},{7,8},{8,9},{9,10... | collective-permute-start | bytes 1572872 | tf_op jit(solution)/shard_map/while/body/eval_jaxpr/ppermute | solution.py:10
  145.8 10.8 %collective-permute-start = (bf16[2,1024,128]{2,1,0:T(8,128)(2,1)S(1)}, bf16[2,1024,128]{2,1,0:T(8,128)(2,1)S(1)}, u32[]{:S(2)}, u32[]{:S(2)}) collective-permute-start(bf16[2,1024,128]{2,1,0:T(8,128)(2,1)S(1)} %copy.44), channel_id=1, source_target_pairs={{15,0},{0,1},{1,2},{2,3},{3,4},{4,5},{5,6},{6,7},{7,8},{8,9},{9,10... | collective-permute-start | bytes 1572872 | tf_op jit(solution)/shard_map/while/body/eval_jaxpr/ppermute | solution.py:10
  156.7 10.8 %collective-permute-start = (bf16[2,1024,128]{2,1,0:T(8,128)(2,1)S(1)}, bf16[2,1024,128]{2,1,0:T(8,128)(2,1)S(1)}, u32[]{:S(2)}, u32[]{:S(2)}) collective-permute-start(bf16[2,1024,128]{2,1,0:T(8,128)(2,1)S(1)} %copy.44), channel_id=1, source_target_pairs={{15,0},{0,1},{1,2},{2,3},{3,4},{4,5},{5,6},{6,7},{7,8},{8,9},{9,10... | collective-permute-start | bytes 1572872 | tf_op jit(solution)/shard_map/while/body/eval_jaxpr/ppermute | solution.py:10
  167.4 5.6 %copy-start.7 = (s32[32]{0:T(128)S(1)}, s32[32]{0:T(128)}, u32[]{:S(2)}) copy-start(s32[32]{0:T(128)} %param.20) | copy-start | bytes 388
  173.3 42.0 %all-to-all-start = ((bf16[16,2,128,128]{3,2,1,0:T(8,128)(2,1)}), bf16[16,2,128,128]{3,2,1,0:T(8,128)(2,1)}, u32[]{:S(2)}, u32[]{:S(2)}) async-start(bf16[16,2,128,128]{3,2,1,0:T(8,128)(2,1)} %bitcast.6), calls=%async_computation | async-start | bytes 2097152 | tf_op jit(solution)/shard_map/all_to_all | solution.py:76
  201.6 69.1 %all-gather.2.cloned.1.call-start = ((), (), s32[]{:S(2)}) async-start(), calls=%async_computation.3 | async-start | bytes 4456448 | tf_op jit(solution)/shard_map/all_gather | solution.py:129
  201.8 16.3 %copy-start.4 = (bf16[2,512,128]{2,1,0:T(8,128)(2,1)S(1)}, bf16[2,512,128]{2,1,0:T(8,128)(2,1)}, u32[]{:S(2)}) copy-start(bf16[2,512,128]{2,1,0:T(8,128)(2,1)} %reshape.304) | copy-start | bytes 786436
  201.8 16.3 %copy-start.5 = (bf16[2,32,128]{2,1,0:T(8,128)(2,1)S(1)}, bf16[2,32,128]{2,1,0:T(8,128)(2,1)}, u32[]{:S(2)}) copy-start(bf16[2,32,128]{2,1,0:T(8,128)(2,1)} %param.13) | copy-start | bytes 49156
  223.4 3.1 copy-start.3
  223.4 3.1 copy-start.6
  231.5 124.1 %reduce-scatter.2.cloned.1.call-start = ((), (), s32[]{:S(2)}) async-start(), calls=%async_computation.4 | async-start | bytes 2359296 | tf_op jit(solution)/shard_map/reduce_scatter | solution.py:132
Sparse Core Ops, SparseCore 0:
  231.6 39.0 all-gather.1
  280.1 75.4 reduce-scatter.1
where the time goes:
time: 364 us; the launch traced here: 362 us
  waiting for transfers between devices  180 us (49%)
  starting transfers between devices  82.5 us (23%)
  matrix products  50.7 us (14%)
  other arithmetic  21.1 us (6%)
  between operations  14.3 us (4%)
  local copies, waits for them, and re-layouts  13 us (4%)
    reduce_scatter x1, waiting for transfers between devices, on_device(): lax.psum_scatter(terms.astype(jnp.bfloat16), 'kvh', scatter_dimension=0,...  75.6 us
    ppermute x15, waiting for transfers between devices, from_behind(): return lax.ppermute(block, axis, route)  59.4 us
    ppermute x15, starting transfers between devices, from_behind(): return lax.ppermute(block, axis, route)  48.2 us
    all_gather x1, waiting for transfers between devices, on_device(): shard_piece = lax.all_gather(heads_out, ('grp', 'blk'), axis=0, tiled=True)  39.2 us
    all_to_all x1, starting transfers between devices, on_device(): lax.all_to_all(pool_keys[local_ids], ('grp', 'blk'), split_axis=0, concat...  28.3 us
    dot_general x16, matrix products, absorb(): jnp.dot(weights.astype(jnp.bfloat16), values, preferred_element_type=jnp....  18.8 us
    reduce_sum x16, other arithmetic, absorb(): total = total * shrink + jnp.sum(weights, axis=1)  13.9 us
    dot_general x16, matrix products, absorb(): jnp.dot(query_rows, keys.T, preferred_element_type=jnp.float32) * factor  13.3 us
  transfers between devices with their start and end apart: 19, of which 13 were waited for; matrix products, arithmetic and copies ran while one was open for 15% of the time, Pallas kernels for 0%

commit v1 on v0

v1 whole, which is shorter than its diff:
```python
import functools
import math

import jax
import jax.numpy as jnp
from jax import lax
from jax.experimental import pallas as pl
from jax.experimental.pallas import tpu as pltpu
from jax.sharding import PartitionSpec as P

F32 = jnp.float32
BF16 = jnp.bfloat16
HEAD = 128
ROWS = 1024
TILE = 512
UNIT = 1024
ONES = 16
LOG2_SCALE = HEAD**-0.5 * math.log2(math.e)
HIDDEN = -1e30
NT = (((1,), (1,)), ((), ()))
VMEM_LIMIT = 60 * 2**20
VMEM = pl.BlockSpec(memory_space=pltpu.VMEM)
SMEM = pl.BlockSpec(memory_space=pltpu.SMEM)


def place():
    kvh, grp, core = lax.axis_index("kvh"), lax.axis_index("grp"), lax.axis_index("blk")
    return kvh, grp // 4, grp % 4, core


def peer(dx, dy, dc):
    kvh, x, y, core = place()
    px = 1 - x if dx else x
    pc = 1 - core if dc else core
    return (kvh, px * 4 + (y + dy) % 4, pc)


def remote(src, dst, send, recv, to):
    return pltpu.make_async_remote_copy(
        src_ref=src,
        dst_ref=dst,
        send_sem=send,
        recv_sem=recv,
        device_id=to,
        device_id_type=pl.DeviceIdType.MESH,
    )


def greet(peers):
    barrier = pltpu.get_barrier_semaphore()
    for to in peers:
        pl.semaphore_signal(barrier, inc=1, device_id=to, device_id_type=pl.DeviceIdType.MESH)
    pl.semaphore_wait(barrier, len(peers))


def turn(i):
    return jnp.where(i == 3, 0, 1 + (2 * i) % 3)


def attention_kernel(
    table,
    q_in,
    new_k,
    new_v,
    pre_k,
    pre_v,
    pool_k,
    pool_v,
    out,
    q_raw,
    q_two,
    kv,
    hist_out,
    hist,
    new_kv,
    top,
    accum,
    score_a,
    score_b,
    part_out,
    part_in,
    lse_out,
    lse_in,
    q_send,
    q_recv,
    kv_send,
    kv_recv,
    hist_send,
    hist_recv,
    part_send,
    part_recv,
    lse_send,
    lse_recv,
):
    kvh, x, y, core = place()
    partner = peer(0, 0, 1)
    scores = (score_a, score_b)

    def holder(t):
        dx, dc = t // 2, t % 2
        return ((1 - x if dx else x) * 4 + y) * 2 + (1 - core if dc else core)

    def entry(first_or_second, owner, request_pair):
        return table[first_or_second * 256 + owner * 16 + request_pair]

    def score(j, keys, tile, mask):
        count = keys.shape[0]
        value = lax.dot_general(
            jnp.concatenate([keys, keys], axis=1),
            q_two[j, tile * TILE : (tile + 1) * TILE, :],
            NT,
            preferred_element_type=F32,
        )
        if mask is None:
            scores[tile][:count] = value
        else:
            for b in range(count // 128):
                rows = slice(b * 128, (b + 1) * 128)
                scores[tile][rows] = jnp.where(mask(b, tile), value[rows], HIDDEN)

    def weigh(j, values, tile, count):
        cols = slice(tile * TILE, (tile + 1) * TILE)
        old = top[j, :, cols]
        newest = jnp.maximum(old, scores[tile][:count].max(axis=0, keepdims=True))
        shrink = jnp.exp2(old - newest)
        top[j, :, cols] = newest
        weights = jnp.exp2(scores[tile][:count] - newest).astype(BF16)
        values = jnp.concatenate([values, jnp.ones((ONES, count), BF16)], axis=0)
        accum[j, :, cols] = accum[j, :, cols] * shrink + jnp.dot(
            values, weights, preferred_element_type=F32
        )

    def absorb(j, parts):
        tasks = [(part, tile) for part in parts for tile in range(2)]
        score(j, tasks[0][0][0](), tasks[0][1], tasks[0][0][2])
        for at, ((keys, values, mask), tile) in enumerate(tasks):
            if at + 1 < len(tasks):
                (after_keys, _, after_mask), after_tile = tasks[at + 1]
                score(j, after_keys(), after_tile, after_mask)
            loaded = values()
            weigh(j, loaded, tile, loaded.shape[1])

    def prefix_part(slot):
        return (
            lambda: jnp.concatenate([kv[slot, 0, b] for b in range(8)], axis=0),
            lambda: jnp.concatenate([kv[slot, 1, b] for b in range(8)], axis=1),
            None,
        )

    def hist_part(j):
        request_pair = (x * 4 + (y + j) % 4) * 2 + core

        def mask(b, tile):
            code = entry(b % 2, holder(b // 2), request_pair)
            lane = lax.broadcasted_iota(jnp.int32, (1, TILE), 1)
            limit = jnp.where((lane // 32) % 2 == (code // 32) % 2, (code // 64) % 256, 0)
            return lax.broadcasted_iota(jnp.int32, (128, TILE), 0) < limit

        return (
            lambda: jnp.concatenate(
                [hist[t, j, 0, i] for t in range(4) for i in range(2)], axis=0
            ),
            lambda: jnp.concatenate(
                [hist[t, j, 1, i] for t in range(4) for i in range(2)], axis=1
            ),
            mask,
        )

    def new_part():
        def mask(b, tile):
            lane = lax.broadcasted_iota(jnp.int32, (128, TILE), 1) % 64
            key = lax.broadcasted_iota(jnp.int32, (128, TILE), 0)
            return (key <= lane) & (key >= (lane // 32) * 32)

        return (lambda: new_kv[0], lambda: new_kv[1], mask)

    def start_state(j):
        q = q_raw[j].astype(F32) * LOG2_SCALE
        high = q.astype(BF16)
        q_two[j, :, :HEAD] = high
        q_two[j, :, HEAD:] = (q - high.astype(F32)).astype(BF16)
        top[j] = jnp.full((1, ROWS), HIDDEN, F32)
        accum[j] = jnp.zeros((HEAD + ONES, ROWS), F32)

    for g in range(16):
        q_raw[0, g * 64 : (g + 1) * 64, :] = q_in[:, g * HEAD : (g + 1) * HEAD]
    for b in range(8):
        kv[0, 0, b] = pre_k[b * 128 : (b + 1) * 128, :]
        kv[0, 1, b] = pre_v[b * 128 : (b + 1) * 128, :].T

    greet([peer(0, 0, 1), peer(1, 0, 0), peer(1, 0, 1), peer(0, 1, 0), peer(0, 2, 0), peer(0, 3, 0)])

    def kv_copy(slot):
        src, to = ((0, partner), (0, peer(1, 0, 0)), (2, partner))[slot - 1]
        return remote(kv.at[src], kv.at[slot], kv_send.at[slot], kv_recv.at[slot], to)

    def q_copy(dy):
        to = peer(0, dy, 0)
        slot = (4 - dy) % 4
        return remote(q_raw.at[0], q_raw.at[slot], q_send.at[slot], q_recv.at[slot], to)

    def hist_copy(t, j):
        return remote(
            hist_out.at[t, j],
            hist.at[t, j],
            hist_send.at[t, j],
            hist_recv.at[t, j],
            peer(t // 2, 0, t % 2),
        )

    def part_copy(j):
        slot = (4 - j) % 4
        to = peer(0, j, 0)
        return (
            remote(part_out.at[j], part_in.at[slot], part_send.at[j], part_recv.at[slot], to),
            remote(lse_out.at[j], lse_in.at[slot], lse_send.at[j], lse_recv.at[slot], to),
        )

    kv_copy(2).start()
    kv_copy(1).start()
    for dy in (1, 3, 2):
        q_copy(dy).start()

    def fill(i, _):
        j = turn(i)
        for t in range(4):
            request_pair = (
                ((1 - x if t // 2 else x) * 4 + (y + j) % 4) * 2 + (1 - core if t % 2 else core)
            )
            own = (x * 4 + y) * 2 + core
            store = hist if t == 0 else hist_out
            for n in range(2):
                local = entry(n, own, request_pair) % 32
                store[t, j, 0, n] = pool_k[local]
                store[t, j, 1, n] = pool_v[local].T
            if t > 0:
                hist_copy(t, j).start()
        return 0

    lax.fori_loop(0, 4, fill, 0)

    start_state(0)
    new_kv[...] = jnp.zeros((2, 128, 128), BF16)
    new_kv[0, :64, :] = new_k[...]
    new_kv[1, :, :] = jnp.concatenate([new_v[...], jnp.zeros((64, HEAD), BF16)], axis=0).T
    absorb(0, [prefix_part(0), new_part()])
    kv_copy(1).wait_recv()
    absorb(0, [prefix_part(1)])

    def near(i, _):
        @pl.when(i == 2)
        def _():
            kv_copy(2).wait_recv()
            kv_copy(3).start()

        j = turn(i)
        remote(q_raw.at[0], q_raw.at[j], q_send.at[j], q_recv.at[j], partner).wait_recv()
        start_state(j)
        absorb(j, [prefix_part(0), prefix_part(1)])
        return 0

    lax.fori_loop(0, 3, near, 0)
    kv_copy(3).wait_recv()

    def far(i, _):
        j = turn(i)
        absorb(j, [prefix_part(2), prefix_part(3)])
        for t in range(1, 4):
            hist_copy(t, j).wait_recv()
        absorb(j, [hist_part(j)])

        @pl.when(i < 3)
        def _():
            total = accum[j, HEAD : HEAD + 1, :]
            part_out[j] = (accum[j, :HEAD, :] / total).astype(BF16)
            lse_out[j] = top[j] + jnp.log2(total)
            for copy in part_copy(j):
                copy.start()

        return 0

    lax.fori_loop(0, 4, far, 0)

    for j in (1, 3, 2):
        remote(part_out.at[j], part_in.at[j], part_send.at[j], part_recv.at[j], partner).wait_recv()
        remote(lse_out.at[j], lse_in.at[j], lse_send.at[j], lse_recv.at[j], partner).wait_recv()

    best = jnp.maximum(jnp.maximum(top[0], lse_in[1]), jnp.maximum(lse_in[2], lse_in[3]))
    own_ratio = jnp.exp2(top[0] - best)
    ratios = [jnp.exp2(lse_in[j] - best) for j in (1, 2, 3)]
    total = accum[0, HEAD : HEAD + 1, :] * own_ratio + ratios[0] + ratios[1] + ratios[2]
    inverse = 1.0 / total
    own_ratio = own_ratio * inverse
    ratios = [r * inverse for r in ratios]
    for g in range(8):
        cols = slice(g * 128, (g + 1) * 128)
        summed = accum[0, :HEAD, cols] * own_ratio[:, cols]
        for j in (1, 2, 3):
            summed = summed + part_in[j, :, cols].astype(F32) * ratios[j - 1][:, cols]
        turned = summed.astype(BF16).T
        out[:, 2 * g * HEAD : (2 * g + 1) * HEAD] = turned[:64]
        out[:, (2 * g + 1) * HEAD : (2 * g + 2) * HEAD] = turned[64:]

    for slot in (1, 2, 3):
        kv_copy(slot).wait_send()
    for dy in (1, 3, 2):
        q_copy(dy).wait_send()
    for t in range(1, 4):
        for j in range(4):
            hist_copy(t, j).wait_send()
    for j in (1, 3, 2):
        for copy in part_copy(j):
            copy.wait_send()


def attention(table, queries, new_k, new_v, pre_k, pre_v, pool_k, pool_v):
    dma = pltpu.SemaphoreType.DMA
    return pl.pallas_call(
        attention_kernel,
        out_shape=jax.ShapeDtypeStruct((64, 2048), BF16),
        in_specs=[SMEM] + [VMEM] * 7,
        out_specs=VMEM,
        scratch_shapes=[
            pltpu.VMEM((4, ROWS, HEAD), BF16),
            pltpu.VMEM((4, ROWS, 2 * HEAD), BF16),
            pltpu.VMEM((4, 2, 8, 128, 128), BF16),
            pltpu.VMEM((4, 4, 2, 2, 128, 128), BF16),
            pltpu.VMEM((4, 4, 2, 2, 128, 128), BF16),
            pltpu.VMEM((2, 128, 128), BF16),
            pltpu.VMEM((4, 1, ROWS), F32),
            pltpu.VMEM((4, HEAD + ONES, ROWS), F32),
            pltpu.VMEM((UNIT, TILE), F32),
            pltpu.VMEM((UNIT, TILE), F32),
            pltpu.VMEM((4, HEAD, ROWS), BF16),
            pltpu.VMEM((4, HEAD, ROWS), BF16),
            pltpu.VMEM((4, 1, ROWS), F32),
            pltpu.VMEM((4, 1, ROWS), F32),
            dma((4,)),
            dma((4,)),
            dma((4,)),
            dma((4,)),
            dma((4, 4)),
            dma((4, 4)),
            dma((4,)),
            dma((4,)),
            dma((4,)),
            dma((4,)),
        ],
        compiler_params=pltpu.CompilerParams(
            collective_id=0, has_side_effects=True, vmem_limit_bytes=VMEM_LIMIT
        ),
        name="attention",
    )(table, queries, new_k, new_v, pre_k, pre_v, pool_k, pool_v)


def projection_kernel(
    heads,
    weight,
    out,
    gathered,
    sums_out,
    sums_in,
    half_out,
    half_in,
    g_send,
    g_recv,
    relay_send,
    relay_recv,
    z_send,
    z_recv,
    h_send,
    h_recv,
):
    kvh, x, y, core = place()
    z, x_hi = kvh // 2, kvh % 2
    grp = x * 4 + y
    partner = peer(0, 0, 1)

    gathered[0, core] = heads[...]
    greet(
        [partner, peer(1, 0, 0), peer(0, 1, 0), peer(0, 2, 0), peer(0, 3, 0)]
        + [(((z + d) % 4) * 2 + x_hi, grp, core) for d in (1, 2, 3)]
        + [(z * 2 + 1 - x_hi, grp, core)]
    )

    def gather_copy(from_slot, dx, dy):
        slot = (from_slot // 4 + dx) * 4 + (4 - dy) % 4
        return remote(
            gathered.at[from_slot, core],
            gathered.at[slot, core],
            g_send.at[slot],
            g_recv.at[slot],
            peer(dx, dy, 0),
        )

    def relay_copy(slot):
        return remote(
            gathered.at[slot, core],
            gathered.at[slot, core],
            relay_send.at[slot],
            relay_recv.at[slot],
            partner,
        )

    def arrived(slot):
        remote(
            gathered.at[0, core], gathered.at[slot, core], g_send.at[slot], g_recv.at[slot], partner
        ).wait_recv()

    def other_arrived(slot):
        remote(
            gathered.at[slot, core],
            gathered.at[slot, 1 - core],
            relay_send.at[slot],
            relay_recv.at[slot],
            partner,
        ).wait_recv()

    def row_block(slot):
        chip = ((1 - x) if slot // 4 else x) * 4 + (y + slot % 4) % 4
        return chip // 2, chip % 2

    def z_copy(slot):
        to_z, parity = row_block(slot)
        away = (z - to_z + 4) % 4
        return remote(
            sums_out.at[slot],
            sums_in.at[away, parity],
            z_send.at[slot],
            z_recv.at[away, parity],
            (to_z * 2 + x_hi, grp, core),
        )

    def multiply(slot):
        rows = jnp.concatenate([gathered[slot, 0], gathered[slot, 1]], axis=0)

        def columns(n, _):
            at = pl.ds(pl.multiple_of(n * 256, 256), 256)
            sums_out[slot, :, at] = jnp.dot(
                rows, weight[:, at], preferred_element_type=F32
            ).astype(BF16)
            return 0

        lax.fori_loop(0, 4, columns, 0)
        to_z, _ = row_block(slot)

        @pl.when(to_z != z)
        def _():
            z_copy(slot).start()

    relay_copy(0).start()
    gather_copy(0, 1, 0).start()
    for dy in (1, 3, 2):
        gather_copy(0, 0, dy).start()
    other_arrived(0)
    multiply(0)
    order = (4, 1, 3, 2, 5, 7, 6)
    for slot in order:
        arrived(slot)
        relay_copy(slot).start()
        if slot == 4:
            for dy in (1, 3, 2):
                gather_copy(4, 0, dy).start()
        other_arrived(slot)
        multiply(slot)

    def own_slot(parity):
        chip = z * 2 + parity
        return jnp.where(chip // 4 == x, 0, 4) + (chip % 4 - y + 4) % 4

    def summed(parity):
        total = sums_out[own_slot(parity)].astype(F32)
        for away in (1, 2, 3):
            remote(
                sums_out.at[0],
                sums_in.at[away, parity],
                z_send.at[0],
                z_recv.at[away, parity],
                partner,
            ).wait_recv()
        for away in (1, 2, 3):
            total = total + sums_in[away, parity].astype(F32)
        return total

    half_copy = remote(
        half_out, half_in, h_send, h_recv, (z * 2 + 1 - x_hi, grp, core)
    )
    half_out[...] = summed(1 - x_hi).astype(BF16)
    half_copy.start()
    mine = summed(x_hi)
    half_copy.wait_recv()
    out[...] = (mine + half_in[...].astype(F32)).astype(BF16)

    half_copy.wait_send()
    relay_copy(0).wait_send()
    for slot in order:
        relay_copy(slot).wait_send()
    gather_copy(0, 1, 0).wait_send()
    for dy in (1, 3, 2):
        gather_copy(0, 0, dy).wait_send()
        gather_copy(4, 0, dy).wait_send()
    for slot in range(8):
        to_z, _ = row_block(slot)

        @pl.when(to_z != z)
        def _():
            z_copy(slot).wait_send()


def projection(heads, weight):
    dma = pltpu.SemaphoreType.DMA
    return pl.pallas_call(
        projection_kernel,
        out_shape=jax.ShapeDtypeStruct((128, 1024), BF16),
        in_specs=[VMEM] * 2,
        out_specs=VMEM,
        scratch_shapes=[
            pltpu.VMEM((8, 2, 64, 2048), BF16),
            pltpu.VMEM((8, 128, 1024), BF16),
            pltpu.VMEM((4, 2, 128, 1024), BF16),
            pltpu.VMEM((128, 1024), BF16),
            pltpu.VMEM((128, 1024), BF16),
            dma((8,)),
            dma((8,)),
            dma((8,)),
            dma((8,)),
            dma((8,)),
            dma((4, 2)),
            dma,
            dma,
        ],
        compiler_params=pltpu.CompilerParams(
            collective_id=1, has_side_effects=True, vmem_limit_bytes=VMEM_LIMIT
        ),
        name="projection",
    )(heads, weight)


def block_table(hist_blocks, hist_len):
    owners = pairs = 16
    ids = hist_blocks.reshape(pairs, 32)
    position = jnp.arange(32, dtype=jnp.int32)
    lengths = jnp.repeat(hist_len.reshape(pairs, 2), 16, axis=1)
    live = jnp.clip(lengths - 128 * (position % 16)[None, :], 0, 128)
    code = position[None, :] * 16384 + live * 64 + (position // 16)[None, :] * 32 + ids % 32
    named = (ids // 32)[None] == jnp.arange(owners, dtype=jnp.int32)[:, None, None]
    first = jnp.min(jnp.where(named, code[None], 2**30), axis=2)
    second = jnp.max(jnp.where(named, code[None], -1), axis=2)
    return jnp.concatenate([first.reshape(-1), second.reshape(-1)])


def on_device(
    queries,
    new_keys,
    new_values,
    prefix_keys,
    prefix_values,
    pool_keys,
    pool_values,
    hist_blocks,
    hist_len,
    out_weight,
):
    table = block_table(hist_blocks, hist_len)
    heads = attention(
        table,
        queries.reshape(64, 2048),
        new_keys.reshape(64, HEAD),
        new_values.reshape(64, HEAD),
        prefix_keys,
        prefix_values,
        pool_keys,
        pool_values,
    )
    projected = projection(heads, out_weight)
    return heads.reshape(2, 32, 2048), projected.reshape(4, 32, 1024)


def solution(mesh):
    in_specs = (
        P(("grp", "blk"), None, "kvh"),
        P(("grp", "blk"), None, "kvh"),
        P(("grp", "blk"), None, "kvh"),
        P(("grp", "blk"), "kvh"),
        P(("grp", "blk"), "kvh"),
        P(("grp", "blk"), None, "kvh"),
        P(("grp", "blk"), None, "kvh"),
        P(),
        P(),
        P("kvh", ("grp", "blk")),
    )
    out_specs = (P(("grp", "blk"), None, "kvh"), P("kvh", None, ("grp", "blk")))
    return jax.shard_map(
        on_device, mesh=mesh, in_specs=in_specs, out_specs=out_specs, check_vma=False
    )
```

time: 364 us -> 116 us (0.32)
  waiting for transfers between devices: 180 us -> 0 us
  Pallas kernels: 0 us -> 110 us
  starting transfers between devices: 82.5 us -> 0 us
  matrix products: 50.7 us -> 0 us
  other arithmetic: 21.1 us -> 1.23 us
  between operations: 14.3 us -> 0.69 us
  local copies, waits for them, and re-layouts: 13 us -> 4.29 us
    pallas_call x0 -> x2, Pallas kernels: none -> 110 us  [the longest x1 67.4 us: projection(): pl.pallas_call(projection_kernel, out_shape=jax.ShapeDtypeStruct((128, 10...]
    reduce_scatter x1 -> x0, waiting for transfers between devices: 75.6 us -> none  [on_device(): lax.psum_scatter(terms.astype(jnp.bfloat16), 'kvh', scatter_dimension=0,...]
    ppermute x15 -> x0, waiting for transfers between devices: 59.4 us -> none  [from_behind(): return lax.ppermute(block, axis, route)]
    dot_general x35 -> x0, matrix products: 50.7 us -> none  [the longest x16 18.8 us: absorb(): jnp.dot(weights.astype(jnp.bfloat16), values, preferred_element_type=jnp....]
    ppermute x15 -> x0, starting transfers between devices: 48.2 us -> none  [from_behind(): return lax.ppermute(block, axis, route)]
    all_gather x1 -> x0, waiting for transfers between devices: 39.2 us -> none  [on_device(): shard_piece = lax.all_gather(heads_out, ('grp', 'blk'), axis=0, tiled=True)]
    all_to_all x2 -> x0, starting transfers between devices: 34.1 us -> none  [the longest x1 28.3 us: on_device(): lax.all_to_all(pool_keys[local_ids], ('grp', 'blk'), split_axis=0, concat...]
    reduce_sum x18 -> x0, other arithmetic: 17.1 us -> none  [the longest x16 13.9 us: absorb(): total = total * shrink + jnp.sum(weights, axis=1)]
  transfers between devices with their start and end apart: 19 -> 0, of which waited for: 13 -> 0; matrix products, arithmetic and copies ran while one was open for 15% -> 0% of each run, Pallas kernels for 0% -> 0%
where the time goes in v1:
time: 116 us
  Pallas kernels  110 us (95%)
  local copies, waits for them, and re-layouts  4.29 us (4%)
  other arithmetic  1.23 us (1%)
    pallas_call x1, Pallas kernels, projection(): pl.pallas_call(projection_kernel, out_shape=jax.ShapeDtypeStruct((128, 10...  67.4 us
    pallas_call x1, Pallas kernels, attention(): pl.pallas_call(attention_kernel, out_shape=jax.ShapeDtypeStruct((64, 2048...  42.2 us
    unnamed x5, local copies, waits for them, and re-layouts  3.15 us

profile of v1, /device:TPU:18, one launch (start us, length us, event | category | flops | bytes accessed | tf_op | source)
XLA Modules:
  0.0 115.8 jit_solution(14712512704092811595)
XLA Ops:
  0.7 0.7 reshape.167
  1.4 0.1 broadcast_in_dim.28
  1.5 0.1 reshape.168
  1.6 0.8 copy.13
  2.3 0.1 reshape.166
  2.4 0.6 select_reduce_fusion.1
  3.0 0.1 reshape.169
  3.1 0.1 reshape.170
  3.2 0.6 pad_add_fusion.table
  3.8 42.2 %attention.1.heads = bf16[64,2048]{1,0:T(8,128)(2,1)} custom-call(s32[512]{0:T(512)} %pad_add_fusion.table, bf16[64,2048]{1,0:T(8,128)(2,1)} %bitcast.7, bf16[64,128]{1,0:T(8,128)(2,1)} %bitcast.8, bf16[64,128]{1,0:T(8,128)(2,1)} %bitcast.9, bf16[1024,128]{1,0:T(8,128)(2,1)} %pre_k.1, bf16[1024,128]{1,0:T(8,128)(2,1)} %pre_v.1, ...), custom_call_target="tpu_custom_call" | custom-call | tf_op jit(solution)/shard_map/attention/pallas_call | solution.py:318
  46.0 0.0 copy-start
  46.0 67.4 %projection.1 = bf16[128,1024]{1,0:T(8,128)(2,1)} custom-call(bf16[64,2048]{1,0:T(8,128)(2,1)} %attention.1.heads, bf16[2048,1024]{1,0:T(8,128)(2,1)} %weight.1), custom_call_target="tpu_custom_call" | custom-call | tf_op jit(solution)/shard_map/projection/pallas_call | solution.py:512
  113.4 0.0 copy-done
  113.4 0.7 copy.16
  114.1 1.7 %copy.17 = bf16[4,32,1024]{2,1,0:T(8,128)(2,1)} copy(bf16[4,32,1024]{2,1,0:T(8,128)(2,1)} %bitcast.6) | data formatting | bytes 524288
  (3 shorter events, 0.0 us)
Async XLA Ops:
  46.0 67.4 %copy-start = (bf16[64,2048]{1,0:T(8,128)(2,1)S(1)}, bf16[64,2048]{1,0:T(8,128)(2,1)}, u32[]{:S(2)}) copy-start(bf16[64,2048]{1,0:T(8,128)(2,1)} %attention.1.heads) | copy-start | bytes 786436

commit v2 on v1

--- a/solution.py
+++ b/solution.py
@@ -18,6 +18,8 @@
 LOG2_SCALE = HEAD**-0.5 * math.log2(math.e)
 HIDDEN = -1e30
 NT = (((1,), (1,)), ((), ()))
+Z_COLS = 512
+X_COLS = 1024 - Z_COLS
 VMEM_LIMIT = 60 * 2**20
 VMEM = pl.BlockSpec(memory_space=pltpu.VMEM)
 SMEM = pl.BlockSpec(memory_space=pltpu.SMEM)
@@ -57,7 +59,7 @@
     return jnp.where(i == 3, 0, 1 + (2 * i) % 3)
 
 
-def attention_kernel(
+def layer_kernel(
     table,
     q_in,
     new_k,
@@ -66,7 +68,11 @@
     pre_v,
     pool_k,
     pool_v,
-    out,
+    weight_in,
+    heads,
+    out_z,
+    out_x,
+    half_in,
     q_raw,
     q_two,
     kv,
@@ -91,9 +97,36 @@
     part_recv,
     lse_send,
     lse_recv,
+    weight,
+    gathered,
+    sums_z,
+    sums_x,
+    z_in,
+    pair_in,
+    merged,
+    merged_in,
+    half_out,
+    w_sem,
+    g_send,
+    g_recv,
+    relay_send,
+    relay_recv,
+    z_send,
+    z_recv,
+    pair_send,
+    pair_recv,
+    m_send,
+    m_recv,
+    h_send,
+    h_recv,
 ):
     kvh, x, y, core = place()
+    z, x_hi = kvh // 2, kvh % 2
+    grp = x * 4 + y
     partner = peer(0, 0, 1)
+    across = (z * 2 + 1 - x_hi, grp, core)
+    weight_copy = pltpu.make_async_copy(weight_in, weight, w_sem)
+    weight_copy.start()
     scores = (score_a, score_b)
 
     def holder(t):
@@ -188,7 +221,10 @@
         kv[0, 0, b] = pre_k[b * 128 : (b + 1) * 128, :]
         kv[0, 1, b] = pre_v[b * 128 : (b + 1) * 128, :].T
 
-    greet([peer(0, 0, 1), peer(1, 0, 0), peer(1, 0, 1), peer(0, 1, 0), peer(0, 2, 0), peer(0, 3, 0)])
+    greet(
+        [partner, peer(1, 0, 0), peer(1, 0, 1), peer(0, 1, 0), peer(0, 2, 0), peer(0, 3, 0), across]
+        + [(((z + d) % 4) * 2 + x_hi, grp, core) for d in (1, 2, 3)]
+    )
 
     def kv_copy(slot):
         src, to = ((0, partner), (0, peer(1, 0, 0)), (2, partner))[slot - 1]
@@ -298,9 +334,206 @@
         for j in (1, 2, 3):
             summed = summed + part_in[j, :, cols].astype(F32) * ratios[j - 1][:, cols]
         turned = summed.astype(BF16).T
-        out[:, 2 * g * HEAD : (2 * g + 1) * HEAD] = turned[:64]
-        out[:, (2 * g + 1) * HEAD : (2 * g + 2) * HEAD] = turned[64:]
-
+        for n in range(2):
+            here = slice((2 * g + n) * HEAD, (2 * g + n + 1) * HEAD)
+            heads[:, here] = turned[n * 64 : (n + 1) * 64]
+            gathered[0, core, :, here] = turned[n * 64 : (n + 1) * 64]
+
+    def gather_copy(from_slot, dx, dy):
+        slot = (from_slot // 4 + dx) * 4 + (from_slot % 4 + 4 - dy) % 4
+        return remote(
+            gathered.at[from_slot, core],
+            gathered.at[slot, core],
+            g_send.at[slot],
+            g_recv.at[slot],
+            peer(dx, dy, 0),
+        )
+
+    def onward(column):
+        from_slot = column * 4 + 3 - 2 * core
+        slot = column * 4 + 2
+        return remote(
+            gathered.at[from_slot, core],
+            gathered.at[slot, core],
+            g_send.at[slot],
+            g_recv.at[slot],
+            peer(0, 1 + 2 * core, 0),
+        )
+
+    def relay_copy(slot):
+        return remote(
+            gathered.at[slot, core],
+            gathered.at[slot, core],
+            relay_send.at[slot],
+            relay_recv.at[slot],
+            partner,
+        )
+
+    def arrived(slot):
+        remote(
+            gathered.at[0, core], gathered.at[slot, core], g_send.at[slot], g_recv.at[slot], partner
+        ).wait_recv()
+        relay_copy(slot).start()
+
+    def row_block(slot):
+        chip = (x + slot // 4) % 2 * 4 + (y + slot % 4) % 4
+        return chip // 2, chip % 2
+
+    def z_copy(slot):
+        to_z, parity = row_block(slot)
+        away = (z - to_z + 4) % 4
+        return remote(
+            sums_z.at[slot],
+            z_in.at[away, parity],
+            z_send.at[slot],
+            z_recv.at[away, parity],
+            (to_z * 2 + x_hi, grp, core),
+        )
+
+    def pair_copy(slot):
+        return remote(
+            sums_x.at[slot], pair_in.at[slot], pair_send.at[slot], pair_recv.at[slot], across
+        )
+
+    def multiply(slot):
+        remote(
+            gathered.at[slot, core],
+            gathered.at[slot, 1 - core],
+            relay_send.at[slot],
+            relay_recv.at[slot],
+            partner,
+        ).wait_recv()
+        rows = jnp.concatenate([gathered[slot, 0], gathered[slot, 1]], axis=0)
+        to_z, parity = row_block(slot)
+
+        for part, (sums, start) in enumerate(((sums_x, Z_COLS), (sums_z, 0))):
+
+            def columns(n, _, sums=sums, start=start):
+                at = pl.ds(pl.multiple_of(n * 256, 256), 256)
+                from_weight = pl.ds(pl.multiple_of(start + n * 256, 256), 256)
+                sums[slot, :, at] = jnp.dot(
+                    rows, weight[:, from_weight], preferred_element_type=F32
+                ).astype(BF16)
+                return 0
+
+            lax.fori_loop(0, sums.shape[2] // 256, columns, 0)
+            if part == 0:
+
+                @pl.when(parity != x_hi)
+                def _():
+                    pair_copy(slot).start()
+
+            else:
+
+                @pl.when(to_z != z)
+                def _():
+                    z_copy(slot).start()
+
+    def merge_slot(i):
+        other = (y + x_hi) % 2
+        return (1 - other) * ((i % 2) * 4 + (i // 2) * 2) + other * (2 * i + 1)
+
+    def merged_copy(slot):
+        to_z, _ = row_block(slot)
+        return remote(
+            merged.at[slot],
+            merged_in.at[(z - to_z + 4) % 4],
+            m_send.at[slot],
+            m_recv.at[(z - to_z + 4) % 4],
+            (to_z * 2 + x_hi, grp, core),
+        )
+
+    def merge(i):
+        slot = merge_slot(i)
+        remote(
+            sums_x.at[slot], pair_in.at[slot], pair_send.at[slot], pair_recv.at[slot], across
+        ).wait_recv()
+        merged[slot] = (sums_x[slot].astype(F32) + pair_in[slot].astype(F32)).astype(BF16)
+        to_z, _ = row_block(slot)
+
+        @pl.when(to_z != z)
+        def _():
+            merged_copy(slot).start()
+
+    relay_copy(0).start()
+    for dx, dy in ((1, 0), (0, 1), (0, 3)):
+        gather_copy(0, dx, dy).start()
+    weight_copy.wait()
+    multiply(0)
+    arrived(4)
+    gather_copy(4, 0, 1).start()
+    gather_copy(4, 0, 3).start()
+    arrived(1)
+    arrived(3)
+    onward(0).start()
+    multiply(4)
+    multiply(1)
+    multiply(3)
+    arrived(5)
+    arrived(7)
+    onward(1).start()
+    merge(0)
+    multiply(5)
+    merge(1)
+    multiply(7)
+    arrived(2)
+    multiply(2)
+    arrived(6)
+    multiply(6)
+    merge(2)
+    merge(3)
+
+    def own_slot(parity):
+        chip = z * 2 + parity
+        return (chip // 4 + x) % 2 * 4 + (chip % 4 - y + 4) % 4
+
+    def z_total(parity):
+        for away in (1, 2, 3):
+            remote(
+                sums_z.at[0], z_in.at[away, parity], z_send.at[0], z_recv.at[away, parity], partner
+            ).wait_recv()
+        total = sums_z[own_slot(parity)].astype(F32)
+        for away in (1, 2, 3):
+            total = total + z_in[away, parity].astype(F32)
+        return total.astype(BF16)
+
+    half_copy = remote(half_out, half_in, h_send, h_recv, across)
+    half_out[...] = z_total(1 - x_hi)
+    half_copy.start()
+    out_z[...] = z_total(x_hi)
+    for away in (1, 2, 3):
+        remote(
+            merged.at[0], merged_in.at[away], m_send.at[0], m_recv.at[away], partner
+        ).wait_recv()
+    total = merged[own_slot(x_hi)].astype(F32)
+    for away in (1, 2, 3):
+        total = total + merged_in[away].astype(F32)
+    out_x[...] = total.astype(BF16)
+    half_copy.wait_recv()
+
+    half_copy.wait_send()
+    for slot in range(8):
+        relay_copy(slot).wait_send()
+        to_z, parity = row_block(slot)
+
+        @pl.when(to_z != z)
+        def _():
+            z_copy(slot).wait_send()
+
+        @pl.when(parity != x_hi)
+        def _():
+            pair_copy(slot).wait_send()
+
+        @pl.when((parity == x_hi) & (to_z != z))
+        def _():
+            merged_copy(slot).wait_send()
+
+    for dx, dy in ((1, 0), (0, 1), (0, 3)):
+        gather_copy(0, dx, dy).wait_send()
+    for dy in (1, 3):
+        gather_copy(4, 0, dy).wait_send()
+    onward(0).wait_send()
+    onward(1).wait_send()
     for slot in (1, 2, 3):
         kv_copy(slot).wait_send()
     for dy in (1, 3, 2):
@@ -313,13 +546,18 @@
             copy.wait_send()
 
 
-def attention(table, queries, new_k, new_v, pre_k, pre_v, pool_k, pool_v):
+def layer(table, queries, new_k, new_v, pre_k, pre_v, pool_k, pool_v, weight):
     dma = pltpu.SemaphoreType.DMA
     return pl.pallas_call(
-        attention_kernel,
-        out_shape=jax.ShapeDtypeStruct((64, 2048), BF16),
-        in_specs=[SMEM] + [VMEM] * 7,
-        out_specs=VMEM,
+        layer_kernel,
+        out_shape=[
+            jax.ShapeDtypeStruct((64, 2048), BF16),
+            jax.ShapeDtypeStruct((128, Z_COLS), BF16),
+            jax.ShapeDtypeStruct((128, X_COLS), BF16),
+            jax.ShapeDtypeStruct((128, Z_COLS), BF16),
+        ],
+        in_specs=[SMEM] + [VMEM] * 7 + [pl.BlockSpec(memory_space=pl.ANY)],
+        out_specs=[VMEM] * 4,
         scratch_shapes=[
             pltpu.VMEM((4, ROWS, HEAD), BF16),
             pltpu.VMEM((4, ROWS, 2 * HEAD), BF16),
@@ -345,195 +583,34 @@
             dma((4,)),
             dma((4,)),
             dma((4,)),
+            pltpu.VMEM((2048, 1024), BF16),
+            pltpu.VMEM((8, 2, 64, 2048), BF16),
+            pltpu.VMEM((8, 128, Z_COLS), BF16),
+            pltpu.VMEM((8, 128, X_COLS), BF16),
+            pltpu.VMEM((4, 2, 128, Z_COLS), BF16),
+            pltpu.VMEM((8, 128, X_COLS), BF16),
+            pltpu.VMEM((8, 128, X_COLS), BF16),
+            pltpu.VMEM((4, 128, X_COLS), BF16),
+            pltpu.VMEM((128, Z_COLS), BF16),
+            dma,
+            dma((8,)),
+            dma((8,)),
+            dma((8,)),
+            dma((8,)),
+            dma((8,)),
+            dma((4, 2)),
+            dma((8,)),
+            dma((8,)),
+            dma((8,)),
+            dma((4,)),
+            dma,
+            dma,
         ],
         compiler_params=pltpu.CompilerParams(
             collective_id=0, has_side_effects=True, vmem_limit_bytes=VMEM_LIMIT
         ),
-        name="attention",
-    )(table, queries, new_k, new_v, pre_k, pre_v, pool_k, pool_v)
-
-
-def projection_kernel(
-    heads,
-    weight,
-    out,
-    gathered,
-    sums_out,
-    sums_in,
-    half_out,
-    half_in,
-    g_send,
-    g_recv,
-    relay_send,
-    relay_recv,
-    z_send,
-    z_recv,
-    h_send,
-    h_recv,
-):
-    kvh, x, y, core = place()
-    z, x_hi = kvh // 2, kvh % 2
-    grp = x * 4 + y
-    partner = peer(0, 0, 1)
-
-    gathered[0, core] = heads[...]
-    greet(
-        [partner, peer(1, 0, 0), peer(0, 1, 0), peer(0, 2, 0), peer(0, 3, 0)]
-        + [(((z + d) % 4) * 2 + x_hi, grp, core) for d in (1, 2, 3)]
-        + [(z * 2 + 1 - x_hi, grp, core)]
-    )
-
-    def gather_copy(from_slot, dx, dy):
-        slot = (from_slot // 4 + dx) * 4 + (4 - dy) % 4
-        return remote(
-            gathered.at[from_slot, core],
-            gathered.at[slot, core],
-            g_send.at[slot],
-            g_recv.at[slot],
-            peer(dx, dy, 0),
-        )
-
-    def relay_copy(slot):
-        return remote(
-            gathered.at[slot, core],
-            gathered.at[slot, core],
-            relay_send.at[slot],
-            relay_recv.at[slot],
-            partner,
-        )
-
-    def arrived(slot):
-        remote(
-            gathered.at[0, core], gathered.at[slot, core], g_send.at[slot], g_recv.at[slot], partner
-        ).wait_recv()
-
-    def other_arrived(slot):
-        remote(
-            gathered.at[slot, core],
-            gathered.at[slot, 1 - core],
-            relay_send.at[slot],
-            relay_recv.at[slot],
-            partner,
-        ).wait_recv()
-
-    def row_block(slot):
-        chip = ((1 - x) if slot // 4 else x) * 4 + (y + slot % 4) % 4
-        return chip // 2, chip % 2
-
-    def z_copy(slot):
-        to_z, parity = row_block(slot)
-        away = (z - to_z + 4) % 4
-        return remote(
-            sums_out.at[slot],
-            sums_in.at[away, parity],
-            z_send.at[slot],
-            z_recv.at[away, parity],
-            (to_z * 2 + x_hi, grp, core),
-        )
-
-    def multiply(slot):
-        rows = jnp.concatenate([gathered[slot, 0], gathered[slot, 1]], axis=0)
-
-        def columns(n, _):
-            at = pl.ds(pl.multiple_of(n * 256, 256), 256)
-            sums_out[slot, :, at] = jnp.dot(
-                rows, weight[:, at], preferred_element_type=F32
-            ).astype(BF16)
-            return 0
-
-        lax.fori_loop(0, 4, columns, 0)
-        to_z, _ = row_block(slot)
-
-        @pl.when(to_z != z)
-        def _():
-            z_copy(slot).start()
-
-    relay_copy(0).start()
-    gather_copy(0, 1, 0).start()
-    for dy in (1, 3, 2):
-        gather_copy(0, 0, dy).start()
-    other_arrived(0)
-    multiply(0)
-    order = (4, 1, 3, 2, 5, 7, 6)
-    for slot in order:
-        arrived(slot)
-        relay_copy(slot).start()
-        if slot == 4:
-            for dy in (1, 3, 2):
-                gather_copy(4, 0, dy).start()
-        other_arrived(slot)
-        multiply(slot)
-
-    def own_slot(parity):
-        chip = z * 2 + parity
-        return jnp.where(chip // 4 == x, 0, 4) + (chip % 4 - y + 4) % 4
-
-    def summed(parity):
-        total = sums_out[own_slot(parity)].astype(F32)
-        for away in (1, 2, 3):
-            remote(
-                sums_out.at[0],
-                sums_in.at[away, parity],
-                z_send.at[0],
-                z_recv.at[away, parity],
-                partner,
-            ).wait_recv()
-        for away in (1, 2, 3):
-            total = total + sums_in[away, parity].astype(F32)
-        return total
-
-    half_copy = remote(
-        half_out, half_in, h_send, h_recv, (z * 2 + 1 - x_hi, grp, core)
-    )
-    half_out[...] = summed(1 - x_hi).astype(BF16)
-    half_copy.start()
-    mine = summed(x_hi)
-    half_copy.wait_recv()
-    out[...] = (mine + half_in[...].astype(F32)).astype(BF16)
-
-    half_copy.wait_send()
-    relay_copy(0).wait_send()
-    for slot in order:
-        relay_copy(slot).wait_send()
-    gather_copy(0, 1, 0).wait_send()
-    for dy in (1, 3, 2):
-        gather_copy(0, 0, dy).wait_send()
-        gather_copy(4, 0, dy).wait_send()
-    for slot in range(8):
-        to_z, _ = row_block(slot)
-
-        @pl.when(to_z != z)
-        def _():
-            z_copy(slot).wait_send()
-
-
-def projection(heads, weight):
-    dma = pltpu.SemaphoreType.DMA
-    return pl.pallas_call(
-        projection_kernel,
-        out_shape=jax.ShapeDtypeStruct((128, 1024), BF16),
-        in_specs=[VMEM] * 2,
-        out_specs=VMEM,
-        scratch_shapes=[
-            pltpu.VMEM((8, 2, 64, 2048), BF16),
-            pltpu.VMEM((8, 128, 1024), BF16),
-            pltpu.VMEM((4, 2, 128, 1024), BF16),
-            pltpu.VMEM((128, 1024), BF16),
-            pltpu.VMEM((128, 1024), BF16),
-            dma((8,)),
-            dma((8,)),
-            dma((8,)),
-            dma((8,)),
-            dma((8,)),
-            dma((4, 2)),
-            dma,
-            dma,
-        ],
-        compiler_params=pltpu.CompilerParams(
-            collective_id=1, has_side_effects=True, vmem_limit_bytes=VMEM_LIMIT
-        ),
-        name="projection",
-    )(heads, weight)
+        name="layer",
+    )(table, queries, new_k, new_v, pre_k, pre_v, pool_k, pool_v, weight)
 
 
 def block_table(hist_blocks, hist_len):
@@ -562,7 +639,7 @@
     out_weight,
 ):
     table = block_table(hist_blocks, hist_len)
-    heads = attention(
+    heads, out_z, out_x, half = layer(
         table,
         queries.reshape(64, 2048),
         new_keys.reshape(64, HEAD),
@@ -571,8 +648,10 @@
         prefix_values,
         pool_keys,
         pool_values,
+        out_weight,
     )
-    projected = projection(heads, out_weight)
+    out_z = (out_z.astype(F32) + half.astype(F32)).astype(BF16)
+    projected = jnp.concatenate([out_z, out_x], axis=1)
     return heads.reshape(2, 32, 2048), projected.reshape(4, 32, 1024)
 
 

time: 116 us -> 96.8 us (0.83)
  Pallas kernels: 110 us -> 88.4 us
  other arithmetic: 1.23 us -> 3.86 us
    pallas_call x2 -> x1, Pallas kernels: 110 us -> 88.4 us  [layer(): pl.pallas_call(layer_kernel, out_shape=[jax.ShapeDtypeStruct((64, 2048),...]
    concatenate x0 -> x1, other arithmetic: none -> 1.63 us  [on_device(): projected = jnp.concatenate([out_z, out_x], axis=1)]
    unnamed x5 -> x2, local copies, waits for them, and re-layouts: 3.15 us -> 2.45 us
where the time goes in v2:
time: 96.8 us; the launch traced here: 96.5 us
  Pallas kernels  88.4 us (91%)
  other arithmetic  3.86 us (4%)
  local copies, waits for them, and re-layouts  3.58 us (4%)
    pallas_call x1, Pallas kernels, layer(): pl.pallas_call(layer_kernel, out_shape=[jax.ShapeDtypeStruct((64, 2048),...  88.4 us
    unnamed x2, local copies, waits for them, and re-layouts  2.45 us

profile of v2, /device:TPU:18, one launch (start us, length us, event | category | flops | bytes accessed | tf_op | source)
XLA Modules:
  0.0 96.5 jit_solution(14055423796703277616)
XLA Ops:
  0.6 0.7 reshape.167
  1.4 0.1 broadcast_in_dim.28
  1.5 0.1 reshape.168
  1.5 0.8 copy.13
  2.3 0.1 reshape.166
  2.4 0.6 select_reduce_fusion.1
  3.0 0.1 reshape.169
  3.1 0.1 reshape.170
  3.2 0.6 pad_add_fusion.table
  3.8 88.4 %layer.1 = (bf16[64,2048]{1,0:T(8,128)(2,1)}, bf16[128,512]{1,0:T(8,128)(2,1)}, bf16[128,512]{1,0:T(8,128)(2,1)}, bf16[128,512]{1,0:T(8,128)(2,1)}) custom-call(s32[512]{0:T(512)} %pad_add_fusion.table, bf16[64,2048]{1,0:T(8,128)(2,1)} %bitcast.7, bf16[64,128]{1,0:T(8,128)(2,1)} %bitcast.8, bf16[64,128]{1,0:T(8,128)(2,1)} %bitcast.9, ...), custom_call_target="tpu_custom_call" | custom-call | tf_op jit(solution)/shard_map/layer/pallas_call | solution.py:551
  92.2 1.0 %add_convert_fusion = bf16[128,512]{1,0:T(8,128)(2,1)S(1)} fusion(bf16[128,512]{1,0:T(8,128)(2,1)} %get-tuple-element.8, bf16[128,512]{1,0:T(8,128)(2,1)} %get-tuple-element.7), kind=kLoop, calls=%fused_computation.1 | loop fusion | flops 262144 | bytes 393216 | tf_op jit(solution)/shard_map/convert_element_type | solution.py:653
  93.2 1.6 %pad_maximum_fusion = bf16[128,1024]{1,0:T(8,128)(2,1)} fusion(bf16[128,512]{1,0:T(8,128)(2,1)} %get-tuple-element.9, bf16[128,512]{1,0:T(8,128)(2,1)S(1)} %add_convert_fusion), kind=kLoop, calls=%fused_computation | loop fusion | flops 524288 | bytes 524288 | tf_op jit(solution)/shard_map/concatenate | solution.py:654
  94.8 1.7 %copy.15 = bf16[2,32,2048]{2,1,0:T(8,128)(2,1)} copy(bf16[2,32,2048]{2,1,0:T(8,128)(2,1)} %bitcast.6) | data formatting | bytes 524288
  (3 shorter events, 0.0 us)

commit v3 on v2

--- a/solution.py
+++ b/solution.py
@@ -22,7 +22,6 @@
 X_COLS = 1024 - Z_COLS
 VMEM_LIMIT = 60 * 2**20
 VMEM = pl.BlockSpec(memory_space=pltpu.VMEM)
-SMEM = pl.BlockSpec(memory_space=pltpu.SMEM)
 
 
 def place():
@@ -48,31 +47,31 @@
     )
 
 
-def greet(peers):
-    barrier = pltpu.get_barrier_semaphore()
-    for to in peers:
-        pl.semaphore_signal(barrier, inc=1, device_id=to, device_id_type=pl.DeviceIdType.MESH)
-    pl.semaphore_wait(barrier, len(peers))
-
-
 def turn(i):
     return jnp.where(i == 3, 0, 1 + (2 * i) % 3)
 
 
 def layer_kernel(
-    table,
-    q_in,
+    blocks,
+    lengths,
     new_k,
     new_v,
+    q_hbm,
     pre_k,
     pre_v,
+    pool_k_hbm,
+    pool_v_hbm,
+    weight_in,
+    heads,
+    out,
+    half_in,
+    q_in,
+    v_in,
     pool_k,
     pool_v,
-    weight_in,
-    heads,
-    out_z,
-    out_x,
-    half_in,
+    table_wide,
+    table,
+    in_sem,
     q_raw,
     q_two,
     kv,
@@ -126,15 +125,51 @@
     partner = peer(0, 0, 1)
     across = (z * 2 + 1 - x_hi, grp, core)
     weight_copy = pltpu.make_async_copy(weight_in, weight, w_sem)
+    inputs = [
+        pltpu.make_async_copy(src, dst, in_sem.at[n])
+        for n, (src, dst) in enumerate(
+            (
+                (pre_k, kv.at[0, 0]),
+                (pre_v, v_in),
+                (q_hbm, q_in),
+                (pool_k_hbm, pool_k),
+                (pool_v_hbm, pool_v),
+            )
+        )
+    ]
+    for copy in inputs:
+        copy.start()
     weight_copy.start()
+    barrier = pltpu.get_barrier_semaphore()
+    peers = [partner, peer(1, 0, 0), peer(1, 0, 1), peer(0, 1, 0), peer(0, 2, 0), peer(0, 3, 0), across]
+    peers += [(((z + d) % 4) * 2 + x_hi, grp, core) for d in (1, 2, 3)]
+    for to in peers:
+        pl.semaphore_signal(barrier, inc=1, device_id=to, device_id_type=pl.DeviceIdType.MESH)
     scores = (score_a, score_b)
 
     def holder(t):
         dx, dc = t // 2, t % 2
         return ((1 - x if dx else x) * 4 + y) * 2 + (1 - core if dc else core)
 
-    def entry(first_or_second, owner, request_pair):
-        return table[first_or_second * 256 + owner * 16 + request_pair]
+    def fill_table():
+        ids = blocks[...]
+        request = lax.broadcasted_iota(jnp.int32, ids.shape, 1)
+        block = lax.broadcasted_iota(jnp.int32, ids.shape, 0)
+        live = jnp.clip(lengths[...] - 128 * block, 0, 128)
+        code = ((request & 1) * 16 + block) * 16384 + live * 64 + (request & 1) * 32 + (ids & 31)
+        for t in range(4):
+            named = (ids >> 5) == holder(t)
+            table_wide[2 * t : 2 * t + 1, :32] = jnp.min(
+                jnp.where(named, code, 2**30), axis=0, keepdims=True
+            )
+            table_wide[2 * t + 1 : 2 * t + 2, :32] = jnp.max(
+                jnp.where(named, code, -1), axis=0, keepdims=True
+            )
+
+    def entry(n, t, request_pair):
+        one = table[2 * t + n, 2 * request_pair]
+        two = table[2 * t + n, 2 * request_pair + 1]
+        return jnp.maximum(one, two) if n else jnp.minimum(one, two)
 
     def score(j, keys, tile, mask):
         count = keys.shape[0]
@@ -184,7 +219,7 @@
         request_pair = (x * 4 + (y + j) % 4) * 2 + core
 
         def mask(b, tile):
-            code = entry(b % 2, holder(b // 2), request_pair)
+            code = entry(b % 2, b // 2, request_pair)
             lane = lax.broadcasted_iota(jnp.int32, (1, TILE), 1)
             limit = jnp.where((lane // 32) % 2 == (code // 32) % 2, (code // 64) % 256, 0)
             return lax.broadcasted_iota(jnp.int32, (128, TILE), 0) < limit
@@ -215,16 +250,16 @@
         top[j] = jnp.full((1, ROWS), HIDDEN, F32)
         accum[j] = jnp.zeros((HEAD + ONES, ROWS), F32)
 
+    fill_table()
+    table_copy = pltpu.make_async_copy(table_wide, table, in_sem.at[5])
+    table_copy.start()
+    for copy in inputs[:3]:
+        copy.wait()
+    for b in range(8):
+        kv[0, 1, b] = v_in[b].T
     for g in range(16):
         q_raw[0, g * 64 : (g + 1) * 64, :] = q_in[:, g * HEAD : (g + 1) * HEAD]
-    for b in range(8):
-        kv[0, 0, b] = pre_k[b * 128 : (b + 1) * 128, :]
-        kv[0, 1, b] = pre_v[b * 128 : (b + 1) * 128, :].T
-
-    greet(
-        [partner, peer(1, 0, 0), peer(1, 0, 1), peer(0, 1, 0), peer(0, 2, 0), peer(0, 3, 0), across]
-        + [(((z + d) % 4) * 2 + x_hi, grp, core) for d in (1, 2, 3)]
-    )
+    pl.semaphore_wait(barrier, len(peers))
 
     def kv_copy(slot):
         src, to = ((0, partner), (0, peer(1, 0, 0)), (2, partner))[slot - 1]
@@ -241,7 +276,7 @@
             hist.at[t, j],
             hist_send.at[t, j],
             hist_recv.at[t, j],
-            peer(t // 2, 0, t % 2),
+            (kvh, (x + t // 2) % 2 * 4 + y, (core + t % 2) % 2),
         )
 
     def part_copy(j):
@@ -257,23 +292,35 @@
     for dy in (1, 3, 2):
         q_copy(dy).start()
 
-    def fill(i, _):
+    def gather_blocks(t, j, store):
+        request_pair = ((x + t // 2) % 2 * 4 + (y + j) % 4) * 2 + (core + t % 2) % 2
+        for n in range(2):
+            local = entry(n, 0, request_pair) & 31
+            store[t, j, 0, n] = pool_k[local]
+            store[t, j, 1, n] = pool_v[local].T
+
+    def send_along_x(lane):
+        def fill(i, _):
+            t, j = 2 + (core + lane) % 2, turn(i)
+            gather_blocks(t, j, hist_out)
+            hist_copy(t, j).start()
+            return 0
+
+        lax.fori_loop(0, 4, fill, 0)
+
+    def send_near(i, _):
         j = turn(i)
-        for t in range(4):
-            request_pair = (
-                ((1 - x if t // 2 else x) * 4 + (y + j) % 4) * 2 + (1 - core if t % 2 else core)
-            )
-            own = (x * 4 + y) * 2 + core
-            store = hist if t == 0 else hist_out
-            for n in range(2):
-                local = entry(n, own, request_pair) % 32
-                store[t, j, 0, n] = pool_k[local]
-                store[t, j, 1, n] = pool_v[local].T
-            if t > 0:
-                hist_copy(t, j).start()
+        gather_blocks(1, j, hist_out)
+        hist_copy(1, j).start()
+        gather_blocks(0, j, hist)
         return 0
 
-    lax.fori_loop(0, 4, fill, 0)
+    for copy in inputs[3:]:
+        copy.wait()
+    table_copy.wait()
+    send_along_x(0)
+    send_along_x(1)
+    lax.fori_loop(0, 4, send_near, 0)
 
     start_state(0)
     new_kv[...] = jnp.zeros((2, 128, 128), BF16)
@@ -299,23 +346,31 @@
     kv_copy(3).wait_recv()
 
     def far(i, _):
-        j = turn(i)
-        absorb(j, [prefix_part(2), prefix_part(3)])
-        for t in range(1, 4):
-            hist_copy(t, j).wait_recv()
-        absorb(j, [hist_part(j)])
-
-        @pl.when(i < 3)
+        is_far = jnp.where(core == 0, 1 - i % 2, 1 - i // 4) == 1
+        order = jnp.where(core == 0, i // 2, i % 4)
+        j = turn(order)
+
+        @pl.when(is_far)
         def _():
-            total = accum[j, HEAD : HEAD + 1, :]
-            part_out[j] = (accum[j, :HEAD, :] / total).astype(BF16)
-            lse_out[j] = top[j] + jnp.log2(total)
-            for copy in part_copy(j):
-                copy.start()
+            absorb(j, [prefix_part(2), prefix_part(3)])
+
+        @pl.when(jnp.logical_not(is_far))
+        def _():
+            for t in range(1, 4):
+                hist_copy(t, j).wait_recv()
+            absorb(j, [hist_part(j)])
+
+            @pl.when(order < 3)
+            def _():
+                total = accum[j, HEAD : HEAD + 1, :]
+                part_out[j] = (accum[j, :HEAD, :] / total).astype(BF16)
+                lse_out[j] = top[j] + jnp.log2(total)
+                for copy in part_copy(j):
+                    copy.start()
 
         return 0
 
-    lax.fori_loop(0, 4, far, 0)
+    lax.fori_loop(0, 8, far, 0)
 
     for j in (1, 3, 2):
         remote(part_out.at[j], part_in.at[j], part_send.at[j], part_recv.at[j], partner).wait_recv()
@@ -395,39 +450,43 @@
             sums_x.at[slot], pair_in.at[slot], pair_send.at[slot], pair_recv.at[slot], across
         )
 
-    def multiply(slot):
-        remote(
-            gathered.at[slot, core],
-            gathered.at[slot, 1 - core],
-            relay_send.at[slot],
-            relay_recv.at[slot],
-            partner,
-        ).wait_recv()
-        rows = jnp.concatenate([gathered[slot, 0], gathered[slot, 1]], axis=0)
-        to_z, parity = row_block(slot)
+    def multiply(slots):
+        for slot in slots:
+            remote(
+                gathered.at[slot, core],
+                gathered.at[slot, 1 - core],
+                relay_send.at[slot],
+                relay_recv.at[slot],
+                partner,
+            ).wait_recv()
+        rows = jnp.concatenate([gathered[slot, n] for slot in slots for n in range(2)], axis=0)
 
         for part, (sums, start) in enumerate(((sums_x, Z_COLS), (sums_z, 0))):
 
             def columns(n, _, sums=sums, start=start):
                 at = pl.ds(pl.multiple_of(n * 256, 256), 256)
                 from_weight = pl.ds(pl.multiple_of(start + n * 256, 256), 256)
-                sums[slot, :, at] = jnp.dot(
+                value = jnp.dot(
                     rows, weight[:, from_weight], preferred_element_type=F32
                 ).astype(BF16)
+                for m, slot in enumerate(slots):
+                    sums[slot, :, at] = value[m * 128 : (m + 1) * 128]
                 return 0
 
             lax.fori_loop(0, sums.shape[2] // 256, columns, 0)
-            if part == 0:
-
-                @pl.when(parity != x_hi)
-                def _():
-                    pair_copy(slot).start()
-
-            else:
-
-                @pl.when(to_z != z)
-                def _():
-                    z_copy(slot).start()
+            for slot in slots:
+                to_z, parity = row_block(slot)
+                if part == 0:
+
+                    @pl.when(parity != x_hi)
+                    def _(slot=slot):
+                        pair_copy(slot).start()
+
+                else:
+
+                    @pl.when(to_z != z)
+                    def _(slot=slot):
+                        z_copy(slot).start()
 
     def merge_slot(i):
         other = (y + x_hi) % 2
@@ -458,30 +517,40 @@
     relay_copy(0).start()
     for dx, dy in ((1, 0), (0, 1), (0, 3)):
         gather_copy(0, dx, dy).start()
+
+    def gather_step(n):
+        if n == 0:
+            arrived(4)
+            gather_copy(4, 0, 1).start()
+            gather_copy(4, 0, 3).start()
+        elif n == 1:
+            arrived(1)
+            arrived(3)
+            onward(0).start()
+        elif n == 2:
+            arrived(5)
+            arrived(7)
+            onward(1).start()
+        else:
+            arrived(2)
+            arrived(6)
+
+    @pl.when(core == 0)
+    def _():
+        for n in range(4):
+            gather_step(n)
+
     weight_copy.wait()
-    multiply(0)
-    arrived(4)
-    gather_copy(4, 0, 1).start()
-    gather_copy(4, 0, 3).start()
-    arrived(1)
-    arrived(3)
-    onward(0).start()
-    multiply(4)
-    multiply(1)
-    multiply(3)
-    arrived(5)
-    arrived(7)
-    onward(1).start()
-    merge(0)
-    multiply(5)
-    merge(1)
-    multiply(7)
-    arrived(2)
-    multiply(2)
-    arrived(6)
-    multiply(6)
-    merge(2)
-    merge(3)
+    for n, slots in enumerate(((0, 4), (1, 3), (5, 7), (2, 6))):
+
+        @pl.when(core == 1)
+        def _(n=n):
+            gather_step(n)
+
+        multiply(slots)
+        if n >= 2:
+            merge(2 * n - 4)
+            merge(2 * n - 3)
 
     def own_slot(parity):
         chip = z * 2 + parity
@@ -500,7 +569,7 @@
     half_copy = remote(half_out, half_in, h_send, h_recv, across)
     half_out[...] = z_total(1 - x_hi)
     half_copy.start()
-    out_z[...] = z_total(x_hi)
+    out[:, :Z_COLS] = z_total(x_hi)
     for away in (1, 2, 3):
         remote(
             merged.at[0], merged_in.at[away], m_send.at[0], m_recv.at[away], partner
@@ -508,7 +577,7 @@
     total = merged[own_slot(x_hi)].astype(F32)
     for away in (1, 2, 3):
         total = total + merged_in[away].astype(F32)
-    out_x[...] = total.astype(BF16)
+    out[:, Z_COLS:] = total.astype(BF16)
     half_copy.wait_recv()
 
     half_copy.wait_send()
@@ -546,19 +615,25 @@
             copy.wait_send()
 
 
-def layer(table, queries, new_k, new_v, pre_k, pre_v, pool_k, pool_v, weight):
+def layer(blocks, lengths, new_k, new_v, queries, pre_k, pre_v, pool_k, pool_v, weight):
     dma = pltpu.SemaphoreType.DMA
     return pl.pallas_call(
         layer_kernel,
         out_shape=[
             jax.ShapeDtypeStruct((64, 2048), BF16),
-            jax.ShapeDtypeStruct((128, Z_COLS), BF16),
-            jax.ShapeDtypeStruct((128, X_COLS), BF16),
+            jax.ShapeDtypeStruct((128, 1024), BF16),
             jax.ShapeDtypeStruct((128, Z_COLS), BF16),
         ],
-        in_specs=[SMEM] + [VMEM] * 7 + [pl.BlockSpec(memory_space=pl.ANY)],
-        out_specs=[VMEM] * 4,
+        in_specs=[VMEM] * 4 + [pl.BlockSpec(memory_space=pl.ANY)] * 6,
+        out_specs=[VMEM] * 3,
         scratch_shapes=[
+            pltpu.VMEM((64, 2048), BF16),
+            pltpu.VMEM((8, 128, HEAD), BF16),
+            pltpu.VMEM((32, 128, HEAD), BF16),
+            pltpu.VMEM((32, 128, HEAD), BF16),
+            pltpu.VMEM((8, 128), jnp.int32),
+            pltpu.SMEM((8, 128), jnp.int32),
+            dma((6,)),
             pltpu.VMEM((4, ROWS, HEAD), BF16),
             pltpu.VMEM((4, ROWS, 2 * HEAD), BF16),
             pltpu.VMEM((4, 2, 8, 128, 128), BF16),
@@ -610,20 +685,23 @@
             collective_id=0, has_side_effects=True, vmem_limit_bytes=VMEM_LIMIT
         ),
         name="layer",
-    )(table, queries, new_k, new_v, pre_k, pre_v, pool_k, pool_v, weight)
-
-
-def block_table(hist_blocks, hist_len):
-    owners = pairs = 16
-    ids = hist_blocks.reshape(pairs, 32)
-    position = jnp.arange(32, dtype=jnp.int32)
-    lengths = jnp.repeat(hist_len.reshape(pairs, 2), 16, axis=1)
-    live = jnp.clip(lengths - 128 * (position % 16)[None, :], 0, 128)
-    code = position[None, :] * 16384 + live * 64 + (position // 16)[None, :] * 32 + ids % 32
-    named = (ids // 32)[None] == jnp.arange(owners, dtype=jnp.int32)[:, None, None]
-    first = jnp.min(jnp.where(named, code[None], 2**30), axis=2)
-    second = jnp.max(jnp.where(named, code[None], -1), axis=2)
-    return jnp.concatenate([first.reshape(-1), second.reshape(-1)])
+    )(blocks, lengths, new_k, new_v, queries, pre_k, pre_v, pool_k, pool_v, weight)
+
+
+def finish_kernel(heads_in, sums, half, heads, out):
+    heads[...] = heads_in[...]
+    out[:, Z_COLS:] = sums[:, Z_COLS:]
+    out[:, :Z_COLS] = (sums[:, :Z_COLS].astype(F32) + half[...].astype(F32)).astype(BF16)
+
+
+def finish(heads, sums, half):
+    return pl.pallas_call(
+        finish_kernel,
+        out_shape=[jax.ShapeDtypeStruct(a.shape, a.dtype) for a in (heads, sums)],
+        in_specs=[VMEM] * 3,
+        out_specs=[VMEM] * 2,
+        name="finish",
+    )(heads, sums, half)
 
 
 def on_device(
@@ -638,20 +716,19 @@
     hist_len,
     out_weight,
 ):
-    table = block_table(hist_blocks, hist_len)
-    heads, out_z, out_x, half = layer(
-        table,
-        queries.reshape(64, 2048),
+    heads, sums, half = layer(
+        hist_blocks.T,
+        hist_len.reshape(1, -1),
         new_keys.reshape(64, HEAD),
         new_values.reshape(64, HEAD),
-        prefix_keys,
-        prefix_values,
+        queries.reshape(64, 2048),
+        prefix_keys.reshape(8, 128, HEAD),
+        prefix_values.reshape(8, 128, HEAD),
         pool_keys,
         pool_values,
         out_weight,
     )
-    out_z = (out_z.astype(F32) + half.astype(F32)).astype(BF16)
-    projected = jnp.concatenate([out_z, out_x], axis=1)
+    heads, projected = finish(heads, sums, half)
     return heads.reshape(2, 32, 2048), projected.reshape(4, 32, 1024)
 
 

time: 96.8 us -> 92 us (0.950); the launches traced: 96.5 us -> 90.6 us
  other arithmetic: 3.86 us -> 0 us
  local copies, waits for them, and re-layouts: 3.58 us -> 0 us
  Pallas kernels: 88.4 us -> 90 us
    unnamed x2 -> x0, local copies, waits for them, and re-layouts: 2.45 us -> none
    concatenate x2 -> x0, other arithmetic: 2.22 us -> none  [the longest x1 1.63 us: on_device(): projected = jnp.concatenate([out_z, out_x], axis=1)]
    pallas_call x0 -> x1, Pallas kernels: none -> 1.87 us  [finish(): pl.pallas_call(finish_kernel, out_shape=[jax.ShapeDtypeStruct(a.shape, a....]
    reshape x5 -> x0, local copies, waits for them, and re-layouts: 1.06 us -> none  [the longest x2 0.83 us: block_table(): lengths = jnp.repeat(hist_len.reshape(pairs, 2), 16, axis=1)]
    convert_element_type x1 -> x0, other arithmetic: 1 us -> none  [on_device(): out_z = (out_z.astype(F32) + half.astype(F32)).astype(BF16)]
where the time goes in v3:
time: 92 us; the launch traced here: 90.6 us
  Pallas kernels  90 us (98%)
    pallas_call x1, Pallas kernels, layer(): pl.pallas_call(layer_kernel, out_shape=[jax.ShapeDtypeStruct((64, 2048),...  88.1 us
    pallas_call x1, Pallas kernels, finish(): pl.pallas_call(finish_kernel, out_shape=[jax.ShapeDtypeStruct(a.shape, a....  1.87 us

profile of v3, /device:TPU:18, one launch (start us, length us, event | category | flops | bytes accessed | tf_op | source)
XLA Modules:
  0.0 90.6 jit_solution(5391589866059918703)
XLA Ops:
  0.6 88.1 %layer.1 = (bf16[64,2048]{1,0:T(8,128)(2,1)}, bf16[128,1024]{1,0:T(8,128)(2,1)}, bf16[128,512]{1,0:T(8,128)(2,1)}) custom-call(s32[16,32]{1,0:T(8,128)} %bitcast.14, s32[1,32]{1,0:T(1,128)} %bitcast.15, bf16[64,128]{1,0:T(8,128)(2,1)} %bitcast.12, bf16[64,128]{1,0:T(8,128)(2,1)} %bitcast.13, bf16[64,2048]{1,0:T(8,128)(2,1)} %bitcast.9, ...), custom_call_target="tpu_custom_call" | custom-call | tf_op jit(solution)/shard_map/layer/pallas_call | solution.py:620
  88.8 1.9 %finish.1 = (bf16[64,2048]{1,0:T(8,128)(2,1)}, bf16[128,1024]{1,0:T(8,128)(2,1)}) custom-call(bf16[64,2048]{1,0:T(8,128)(2,1)} %get-tuple-element.7.heads_in, bf16[128,1024]{1,0:T(8,128)(2,1)} %get-tuple-element.8.sums, bf16[128,512]{1,0:T(8,128)(2,1)} %get-tuple-element.9.half), custom_call_target="tpu_custom_call" | custom-call | tf_op jit(solution)/shard_map/finish/pallas_call | solution.py:698

commit v4 on v3

--- a/solution.py
+++ b/solution.py
@@ -464,8 +464,8 @@
         for part, (sums, start) in enumerate(((sums_x, Z_COLS), (sums_z, 0))):
 
             def columns(n, _, sums=sums, start=start):
-                at = pl.ds(pl.multiple_of(n * 256, 256), 256)
-                from_weight = pl.ds(pl.multiple_of(start + n * 256, 256), 256)
+                at = pl.ds(pl.multiple_of(n * 512, 512), 512)
+                from_weight = pl.ds(pl.multiple_of(start + n * 512, 512), 512)
                 value = jnp.dot(
                     rows, weight[:, from_weight], preferred_element_type=F32
                 ).astype(BF16)
@@ -473,7 +473,7 @@
                     sums[slot, :, at] = value[m * 128 : (m + 1) * 128]
                 return 0
 
-            lax.fori_loop(0, sums.shape[2] // 256, columns, 0)
+            lax.fori_loop(0, sums.shape[2] // 512, columns, 0)
             for slot in slots:
                 to_z, parity = row_block(slot)
                 if part == 0:
@@ -531,8 +531,8 @@
             arrived(5)
             arrived(7)
             onward(1).start()
+            arrived(2)
         else:
-            arrived(2)
             arrived(6)
 
     @pl.when(core == 0)
@@ -541,13 +541,14 @@
             gather_step(n)
 
     weight_copy.wait()
-    for n, slots in enumerate(((0, 4), (1, 3), (5, 7), (2, 6))):
+    for n, slots in enumerate(((), (0, 4, 1, 3), (2, 5, 7), (6,))):
 
         @pl.when(core == 1)
         def _(n=n):
             gather_step(n)
 
-        multiply(slots)
+        if slots:
+            multiply(slots)
         if n >= 2:
             merge(2 * n - 4)
             merge(2 * n - 3)

time: 92 us -> 91.1 us (level); the launches traced: 90.6 us -> 90.9 us
  no operation moved by 1% of the time
where the time goes in v4:
time: 91.1 us; the launch traced here: 90.9 us
  Pallas kernels  90.3 us (99%)
    pallas_call x1, Pallas kernels, layer(): pl.pallas_call(layer_kernel, out_shape=[jax.ShapeDtypeStruct((64, 2048),...  88.4 us
    pallas_call x1, Pallas kernels, finish(): pl.pallas_call(finish_kernel, out_shape=[jax.ShapeDtypeStruct(a.shape, a....  1.87 us

profile of v4, /device:TPU:18, one launch (start us, length us, event | category | flops | bytes accessed | tf_op | source)
XLA Modules:
  0.0 90.9 jit_solution(16816026093399565783)
XLA Ops:
  0.6 88.4 %layer.1 = (bf16[64,2048]{1,0:T(8,128)(2,1)}, bf16[128,1024]{1,0:T(8,128)(2,1)}, bf16[128,512]{1,0:T(8,128)(2,1)}) custom-call(s32[16,32]{1,0:T(8,128)} %bitcast.14, s32[1,32]{1,0:T(1,128)} %bitcast.15, bf16[64,128]{1,0:T(8,128)(2,1)} %bitcast.12, bf16[64,128]{1,0:T(8,128)(2,1)} %bitcast.13, bf16[64,2048]{1,0:T(8,128)(2,1)} %bitcast.9, ...), custom_call_target="tpu_custom_call" | custom-call | tf_op jit(solution)/shard_map/layer/pallas_call | solution.py:621
  89.0 1.9 %finish.1 = (bf16[64,2048]{1,0:T(8,128)(2,1)}, bf16[128,1024]{1,0:T(8,128)(2,1)}) custom-call(bf16[64,2048]{1,0:T(8,128)(2,1)} %get-tuple-element.7.heads_in, bf16[128,1024]{1,0:T(8,128)(2,1)} %get-tuple-element.8.sums, bf16[128,512]{1,0:T(8,128)(2,1)} %get-tuple-element.9.half), custom_call_target="tpu_custom_call" | custom-call | tf_op jit(solution)/shard_map/finish/pallas_call | solution.py:699

commit v5 on v4

--- a/solution.py
+++ b/solution.py
@@ -549,9 +549,9 @@
 
         if slots:
             multiply(slots)
-        if n >= 2:
-            merge(2 * n - 4)
-            merge(2 * n - 3)
+        if n == 2:
+            merge(0)
+            merge(1)
 
     def own_slot(parity):
         chip = z * 2 + parity
@@ -568,8 +568,24 @@
         return total.astype(BF16)
 
     half_copy = remote(half_out, half_in, h_send, h_recv, across)
-    half_out[...] = z_total(1 - x_hi)
-    half_copy.start()
+    last_is_own = (y + x_hi) % 2 == 0
+
+    def send_half():
+        half_out[...] = z_total(1 - x_hi)
+        half_copy.start()
+
+    @pl.when(last_is_own)
+    def _():
+        send_half()
+        merge(2)
+        merge(3)
+
+    @pl.when(jnp.logical_not(last_is_own))
+    def _():
+        merge(2)
+        merge(3)
+        send_half()
+
     out[:, :Z_COLS] = z_total(x_hi)
     for away in (1, 2, 3):
         remote(

time: 91.1 us -> 91.1 us (level)
  no operation moved by 1% of the time
where the time goes in v5:
time: 91.1 us; the launch traced here: 90.9 us
  Pallas kernels  90.3 us (99%)
    pallas_call x1, Pallas kernels, layer(): pl.pallas_call(layer_kernel, out_shape=[jax.ShapeDtypeStruct((64, 2048),...  88.4 us
    pallas_call x1, Pallas kernels, finish(): pl.pallas_call(finish_kernel, out_shape=[jax.ShapeDtypeStruct(a.shape, a....  1.87 us

profile of v5, /device:TPU:18, one launch (start us, length us, event | category | flops | bytes accessed | tf_op | source)
XLA Modules:
  0.0 90.9 jit_solution(8367791578168676796)
XLA Ops:
  0.6 88.4 %layer.1 = (bf16[64,2048]{1,0:T(8,128)(2,1)}, bf16[128,1024]{1,0:T(8,128)(2,1)}, bf16[128,512]{1,0:T(8,128)(2,1)}) custom-call(s32[16,32]{1,0:T(8,128)} %bitcast.14, s32[1,32]{1,0:T(1,128)} %bitcast.15, bf16[64,128]{1,0:T(8,128)(2,1)} %bitcast.12, bf16[64,128]{1,0:T(8,128)(2,1)} %bitcast.13, bf16[64,2048]{1,0:T(8,128)(2,1)} %bitcast.9, ...), custom_call_target="tpu_custom_call" | custom-call | tf_op jit(solution)/shard_map/layer/pallas_call | solution.py:637
  89.0 1.9 %finish.1 = (bf16[64,2048]{1,0:T(8,128)(2,1)}, bf16[128,1024]{1,0:T(8,128)(2,1)}) custom-call(bf16[64,2048]{1,0:T(8,128)(2,1)} %get-tuple-element.7.heads_in, bf16[128,1024]{1,0:T(8,128)(2,1)} %get-tuple-element.8.sums, bf16[128,512]{1,0:T(8,128)(2,1)} %get-tuple-element.9.half), custom_call_target="tpu_custom_call" | custom-call | tf_op jit(solution)/shard_map/finish/pallas_call | solution.py:715
